TPU v7x, 256 devices: a whole 4x4x8 slice. The times are simulated.
256 devices in a mesh: tp: 4 (over x_lo, core), blk: 64 (over z, y, x_hi).
Axes of the slice: x: 4 (x_hi: 2, x_lo: 2; x = x_hi * 2 + x_lo), y: 4, z: 8, core: 2. Of those that a mesh axis runs over, the one named last changes fastest.
Arguments:
- query_feat: bfloat16 [16384, 768], P('blk', 'tp'), may hold values from -48 to 48
- key_feat: bfloat16 [16384, 768], P('blk', 'tp'), may hold values from -12 to 12
- head_weight: bfloat16 [768, 512], P('tp'), may hold values from -0.21875 to 0.21875
- pair: int32 [16384], P('blk'), may hold values from 0 to 16383, each once
Outputs:
- loss: float32 [], replicated
- grad_query: bfloat16 [16384, 768], P('blk', 'tp')
- grad_key: bfloat16 [16384, 768], P('blk', 'tp')
- grad_head: float32 [768, 512], P('tp')
Inputs may be any that keep to these rules, and one draw needn't show every extreme that they name: pair is a permutation of the 16384 sample indices.
All inputs are finite; a program needn't handle non-finite values.
Results may differ from a plain program's by a relative error of at most 0.0079.
The roundings to bfloat16 on the way count: a program that leaves them out, or rounds other values in their place, can miss the bound.
Values may be sent and summed in bfloat16 or wider, within the bound.
A program may use at most 64 MiB of HBM per device.

v0:
```python
import math

import jax
import jax.numpy as jnp
from jax import lax
from jax.sharding import PartitionSpec as P

logit_gain = 3.0


def shifted(block, axis, distance):
    devices = range(lax.axis_size(axis))
    route = [((i - distance) % len(devices), i) for i in devices]
    return lax.ppermute(block, axis, route)


def combined_all(value, axis, join):
    pieces = jax.tree.map(lambda part: lax.all_gather(part, axis), value)
    head = jax.tree.map(lambda part: part[0], pieces)
    tail = jax.tree.map(lambda part: part[1:], pieces)
    subtotal, _ = lax.scan(lambda subtotal, slab: (join(subtotal, slab), None), head, tail)
    return subtotal


def tile_scores(queries, block, logit_scale):
    return logit_scale * lax.dot_general(
        queries, block, (((1,), (1,)), ((), ())), preferred_element_type=jnp.float32
    )


def combine_stats(first, second):
    new_top = jnp.maximum(first[0], second[0])
    summed = first[1] * jnp.exp(first[0] - new_top) + second[1] * jnp.exp(second[0] - new_top)
    return (new_top, summed, first[2] + second[2])


def body(query_feat, key_feat, head_weight, pair):
    row_count = query_feat.shape[0]
    embed_width = head_weight.shape[1]
    cycle_size = lax.axis_size("blk")
    tp_size = lax.axis_size("tp")
    batch_total = row_count * cycle_size
    quarter = row_count // tp_size
    logit_scale = logit_gain / math.sqrt(embed_width)
    blk_index = lax.axis_index("blk")
    tp_index = lax.axis_index("tp")
    zq_part = jnp.dot(query_feat, head_weight, preferred_element_type=jnp.float32)
    zk_part = jnp.dot(key_feat, head_weight, preferred_element_type=jnp.float32)
    zq_full, zk_full = lax.psum((zq_part, zk_part), "tp")
    zq = zq_full.astype(jnp.bfloat16)
    zk = zk_full.astype(jnp.bfloat16)
    own_block = lax.dynamic_slice_in_dim(zk, tp_index * quarter, quarter, 0)
    local_ids = jnp.arange(quarter, dtype=jnp.int32)

    def block_ids(step_index):
        source = (blk_index - step_index) % cycle_size
        return (source, source * row_count + tp_index * quarter + local_ids)

    def onward(carried):
        return shifted(carried, "blk", 1)

    def onward_again(carried):
        return shifted(carried, "blk", 1)

    def forward_step(step_index, state_in):
        row_top, row_sum, positive, carried = state_in
        source, key_ids = block_ids(step_index)
        key_block = carried
        scores = tile_scores(zq, key_block, logit_scale)
        onehot = pair[:, None] == key_ids[None, :]
        new_top = jnp.maximum(row_top, jnp.max(scores, axis=1))
        row_sum = row_sum * jnp.exp(row_top - new_top) + jnp.sum(
            jnp.exp(scores - new_top[:, None]), axis=1
        )
        positive = positive + jnp.sum(jnp.where(onehot, scores, 0.0), axis=1)
        carried = onward(carried)
        return (new_top, row_sum, positive, carried)

    init = (
        jnp.full((row_count,), -1e30, jnp.float32),
        jnp.zeros((row_count,), jnp.float32),
        jnp.zeros((row_count,), jnp.float32),
        own_block,
    )
    row_top, row_sum, positive, _ = lax.fori_loop(0, cycle_size, forward_step, init)
    row_top, row_sum, positive = combined_all((row_top, row_sum, positive), "tp", combine_stats)
    lse = row_top + jnp.log(row_sum)
    loss_part = jnp.sum(lse - positive)

    def tile_weights(key_block, key_ids):
        scores = tile_scores(zq, key_block, logit_scale)
        onehot = (pair[:, None] == key_ids[None, :]).astype(jnp.float32)
        return ((jnp.exp(scores - lse[:, None]) - onehot) / batch_total).astype(jnp.bfloat16)

    def query_term(weights, key_block):
        return logit_scale * jnp.dot(weights, key_block, preferred_element_type=jnp.float32)

    def key_term(weights):
        return logit_scale * lax.dot_general(
            weights, zq, (((0,), (0,)), ((), ())), preferred_element_type=jnp.float32
        )

    zero_rows = jnp.zeros((row_count, embed_width), jnp.float32)

    def backward_step(step_index, state_in):
        grad_rows, carried, key_grad = state_in
        source, key_ids = block_ids(step_index)
        key_block = carried
        weights = tile_weights(key_block, key_ids)
        grad_rows = grad_rows + query_term(weights, key_block)
        key_grad = key_grad + key_term(weights)
        carried = onward_again(carried)
        key_grad = shifted(key_grad, "blk", 1)
        return (grad_rows, carried, key_grad)

    start = (zero_rows, own_block, jnp.zeros((quarter, embed_width), jnp.float32))
    grad_rows, _, key_grad = lax.fori_loop(0, cycle_size, backward_step, start)
    dzq = lax.psum(grad_rows, "tp").astype(jnp.bfloat16)
    dzk = lax.all_gather(key_grad.astype(jnp.bfloat16), "tp", axis=0, tiled=True)
    back_dims = (((1,), (1,)), ((), ()))
    grad_query = lax.dot_general(
        dzq, head_weight, back_dims, preferred_element_type=jnp.float32
    ).astype(jnp.bfloat16)
    grad_key = lax.dot_general(
        dzk, head_weight, back_dims, preferred_element_type=jnp.float32
    ).astype(jnp.bfloat16)
    row_dims = (((0,), (0,)), ((), ()))
    head_part = lax.dot_general(
        query_feat, dzq, row_dims, preferred_element_type=jnp.float32
    ) + lax.dot_general(key_feat, dzk, row_dims, preferred_element_type=jnp.float32)
    grad_head, loss_total = lax.psum((head_part, loss_part), "blk")
    loss = loss_total / batch_total
    return (loss, grad_query, grad_key, grad_head)


def solution(mesh):
    in_specs = (P("blk", "tp"), P("blk", "tp"), P("tp", None), P("blk"))
    out_specs = (P(), P("blk", "tp"), P("blk", "tp"), P("tp", None))
    return jax.shard_map(body, mesh=mesh, in_specs=in_specs, out_specs=out_specs, check_vma=False)
```

profile of v0, /device:TPU:2, one launch (start us, length us, event | category | flops | bytes accessed | tf_op | source)
XLA Modules:
  0.0 2155.5 jit_solution(3798739706704805455)
XLA Ops:
  9.5 26.2 %all-reduce.6 = (bf16[256,512]{1,0:T(8,128)(2,1)S(1)}, bf16[256,512]{1,0:T(8,128)(2,1)S(1)}) all-reduce(f32[256,512]{1,0:T(8,128)S(1)} %fusion.18, f32[256,512]{1,0:T(8,128)S(1)} %fusion.19), channel_id=1, replica_groups=mesh['tp'=4,'blk'=64] {'tp'}, use_global_device_ids=true, to_apply=%region_0.0 | all-reduce | flops 262144 | bytes 1572864 | tf_op jit(solution)/shard_map/psum | solution.py:49
  36.4 644.2 %while.57 = (s32[]{:T(128)}, f32[256]{0:T(256)S(1)}, f32[256]{0:T(256)S(1)}, f32[256]{0:T(256)S(1)}, bf16[64,512]{1,0:T(8,128)(2,1)S(1)}, /*index=5*/bf16[256,51...) while((s32[]{:T(128)}, f32[256]{0:T(256)S(1)}, ...), condition=%wide.region_6.7_spmd.clone, body=%wide.region_2.6_spmd.clone.sunk | while | flops 16893504 | bytes 871245 | solution.py:85
  38.6 10.0 collective-permute-done
  119.0 9.9 collective-permute-done
  199.3 9.9 collective-permute-done
  279.6 10.0 collective-permute-done
  359.9 9.9 collective-permute-done
  440.2 9.9 collective-permute-done
  520.5 10.0 collective-permute-done
  600.8 9.9 collective-permute-done
  701.3 756.9 %while.58 = (s32[]{:T(128)}, f32[256,512]{1,0:T(8,128)S(1)}, bf16[64,512]{1,0:T(8,128)(2,1)S(1)}, f32[64,512]{1,0:T(8,128)S(1)}, bf16[256,512]{1,0:T(8,128)(2,1)...) while((s32[]{:T(128)}, f32[256,512]{1,0:T(8,128)S(1)}, ...), condition=%wide.region_12.13_spmd.clone, body=%wide.region_11.12_spmd.clone.sunk | while | flops 50905168 | bytes 2984820 | solution.py:117
  715.1 9.8 collective-permute-done.1
  808.0 9.8 collective-permute-done.1
  821.4 9.8 collective-permute-done.1
  927.2 9.8 collective-permute-done.1
  940.1 9.8 collective-permute-done.1
  1033.0 9.8 collective-permute-done.1
  1046.4 9.8 collective-permute-done.1
  1165.2 9.9 collective-permute-done.1
  1258.1 9.8 collective-permute-done.1
  1271.6 9.8 collective-permute-done.1
  1458.1 16.5 all-reduce.7
  1481.9 179.8 %psum.37 = f32[]{:T(128)} all-reduce(f32[]{:T(128)} %get-tuple-element.664), channel_id=1, replica_groups=mesh['tp'=4,'blk'=64] {'blk'}, use_global_device_ids=true, to_apply=%region_10.11 | all-reduce | flops 1 | bytes 8 | tf_op jit(solution)/shard_map/psum | solution.py:131
  1664.0 481.7 %all-reduce.5.cloned.1.call-done = f32[192,512]{1,0:T(8,128)} async-done(((f32[192,512]{1,0:T(8,128)}), f32[192,512]{1,0:T(8,128)}) %all-reduce.5.cloned.1.call-update) | async-done | bytes 393232 | tf_op jit(solution)/shard_map/psum | solution.py:131
  (1198 shorter events, 1249.3 us)
Async XLA Ops:
  7.2 2138.6 %all-reduce.5.cloned.1.call-start = ((), (), s32[]{:S(2)}) async-start(), calls=%async_computation | async-start | bytes 786432 | tf_op jit(solution)/shard_map/psum | solution.py:131
  36.4 12.2 collective-permute-start
  701.8 12.4 collective-permute-start.2
  714.7 11.6 collective-permute-start.2
  795.1 12.1 collective-permute-start.2
  807.6 12.9 collective-permute-start.2
  821.0 12.0 collective-permute-start.2
  902.1 11.3 collective-permute-start.2
  913.8 12.5 collective-permute-start.2
  926.8 12.5 collective-permute-start.2
  939.7 11.7 collective-permute-start.2
  1020.2 12.0 collective-permute-start.2
  1032.6 12.9 collective-permute-start.2
  1046.0 12.1 collective-permute-start.2
  1058.6 11.2 collective-permute-start.2
  1138.9 12.4 collective-permute-start.2
  1151.8 12.5 collective-permute-start.2
  1164.8 11.8 collective-permute-start.2
  1245.4 11.9 collective-permute-start.2
  1257.7 13.0 collective-permute-start.2
  1271.2 12.2 collective-permute-start.2
  1283.8 11.4 collective-permute-start.2
  1364.2 12.3 collective-permute-start.2
  1376.9 12.7 collective-permute-start.2
  (182 other events, 1756.5 us)
Sparse Core Ops, SparseCore 0:
  1482.0 663.7 all-reduce.4
where the time goes:
time: 2160 us
  waiting for transfers between devices  1800 us (83%)
  blocking collectives  244 us (11%)
  matrix products  61.8 us (3%)
    ppermute x192, waiting for transfers between devices, shifted(): return lax.ppermute(block, axis, route)  1320 us
    psum x1, waiting for transfers between devices, body(): grad_head, loss_total = lax.psum((head_part, loss_part), 'blk')  482 us
    psum x1, blocking collectives, body(): grad_head, loss_total = lax.psum((head_part, loss_part), 'blk')  180 us
  transfers between devices with their start and end apart: 193, of which 193 were waited for; matrix products, arithmetic and copies ran while one was open for 3% of the time, Pallas kernels for 0%

commit v1 on v0

v1 whole, which is shorter than its diff:
```python
import math

import jax
import jax.numpy as jnp
from jax import lax
from jax.sharding import Mesh, PartitionSpec as P

logit_gain = 3.0
TP = ("xlo", "core")
BLK = ("z", "y", "xh")
QG = ("z", "core")
KG = ("y", "xh", "xlo")


def body(query_feat, key_feat, head_weight, pair):
    rows = query_feat.shape[0]
    emb = head_weight.shape[1]
    tp_size = lax.axis_size(TP)
    quarter = rows // tp_size
    batch = rows * lax.axis_size(BLK)
    scale = logit_gain / math.sqrt(emb)
    tp_index = lax.axis_index(TP)
    zq_part = jnp.dot(query_feat, head_weight, preferred_element_type=jnp.float32)
    zk_part = jnp.dot(key_feat, head_weight, preferred_element_type=jnp.float32)
    zq_own = lax.psum_scatter(zq_part, TP, scatter_dimension=0, tiled=True).astype(jnp.bfloat16)
    zk_own = lax.psum_scatter(zk_part, TP, scatter_dimension=0, tiled=True).astype(jnp.bfloat16)
    pair_own = lax.dynamic_slice_in_dim(pair, tp_index * quarter, quarter, 0)
    zq = lax.all_gather(zq_own, QG, axis=0, tiled=True)
    zk = lax.all_gather(zk_own, KG, axis=0, tiled=True)
    pair_all = lax.all_gather(pair_own, QG, axis=0, tiled=True)
    local = jnp.arange(quarter, dtype=jnp.int32)
    ys = lax.axis_size("y")
    xhs = lax.axis_size("xh")
    xls = lax.axis_size("xlo")
    y_i = jnp.arange(ys, dtype=jnp.int32)[:, None, None, None]
    xh_i = jnp.arange(xhs, dtype=jnp.int32)[None, :, None, None]
    xl_i = jnp.arange(xls, dtype=jnp.int32)[None, None, :, None]
    z = lax.axis_index("z")
    core = lax.axis_index("core")
    cores = lax.axis_size("core")
    key_ids = (((z * ys + y_i) * xhs + xh_i) * rows + (xl_i * cores + core) * quarter + local).reshape(-1)
    scores = scale * lax.dot_general(zq, zk, (((1,), (1,)), ((), ())), preferred_element_type=jnp.float32)
    onehot = pair_all[:, None] == key_ids[None, :]
    top = jnp.max(scores, axis=1)
    expo = jnp.exp(scores - top[:, None])
    lse_part = top + jnp.log(jnp.sum(expo, axis=1))
    pos_part = jnp.sum(jnp.where(onehot, scores, 0.0))
    lse_parts = lax.all_gather(lse_part, QG, axis=0)
    lse = jax.nn.logsumexp(lse_parts, axis=0)
    loss_part = jnp.sum(lse) / lax.axis_size(QG) - pos_part
    weights = (jnp.exp(scores - lse[:, None]) - onehot.astype(jnp.float32)).astype(jnp.bfloat16)
    factor = scale / batch
    dzq_part = factor * jnp.dot(weights, zk, preferred_element_type=jnp.float32)
    dzk_part = factor * lax.dot_general(weights, zq, (((0,), (0,)), ((), ())), preferred_element_type=jnp.float32)
    dzq_own = lax.psum_scatter(dzq_part, QG, scatter_dimension=0, tiled=True).astype(jnp.bfloat16)
    dzk_own = lax.psum_scatter(dzk_part, KG, scatter_dimension=0, tiled=True).astype(jnp.bfloat16)
    dzq = lax.all_gather(dzq_own, TP, axis=0, tiled=True)
    dzk = lax.all_gather(dzk_own, TP, axis=0, tiled=True)
    back = (((1,), (1,)), ((), ()))
    grad_query = lax.dot_general(dzq, head_weight, back, preferred_element_type=jnp.float32).astype(jnp.bfloat16)
    grad_key = lax.dot_general(dzk, head_weight, back, preferred_element_type=jnp.float32).astype(jnp.bfloat16)
    rowd = (((0,), (0,)), ((), ()))
    head_part = lax.dot_general(query_feat, dzq, rowd, preferred_element_type=jnp.float32) + lax.dot_general(
        key_feat, dzk, rowd, preferred_element_type=jnp.float32
    )
    grad_head = lax.psum(head_part, BLK)
    loss = lax.psum(loss_part, BLK + TP) / batch
    return (loss, grad_query, grad_key, grad_head)


def solution(mesh):
    fine = Mesh(mesh.devices.reshape(2, 2, 8, 4, 2) if mesh.axis_names[0] == "tp" else
                mesh.devices.reshape(8, 4, 2, 2, 2),
                TP + BLK if mesh.axis_names[0] == "tp" else BLK + TP)
    in_specs = (P(BLK, TP), P(BLK, TP), P(TP, None), P(BLK))
    out_specs = (P(), P(BLK, TP), P(BLK, TP), P(TP, None))
    return jax.shard_map(body, mesh=fine, in_specs=in_specs, out_specs=out_specs, check_vma=False)
```

time: 2160 us -> 1000 us (0.46)
  waiting for transfers between devices: 1800 us -> 831 us
  blocking collectives: 244 us -> 118 us
  matrix products: 61.8 us -> 19.7 us
    ppermute x192 -> x0, waiting for transfers between devices: 1320 us -> none  [shifted(): return lax.ppermute(block, axis, route)]
    psum x1, waiting for transfers between devices: 482 us -> 664 us  [body(): grad_head = lax.psum(head_part, BLK)]
    psum x3 -> x1, blocking collectives: 222 us -> 74.4 us  [body(): loss = lax.psum(loss_part, BLK + TP) / batch]
    reduce_scatter x0 -> x4, waiting for transfers between devices: none -> 93.2 us  [the longest x1 49.6 us: body(): lax.psum_scatter(dzk_part, KG, scatter_dimension=0, tiled=True)]
    all_gather x0 -> x2, waiting for transfers between devices: none -> 73.2 us  [the longest x1 48.9 us: body(): zk = lax.all_gather(zk_own, KG, axis=0, tiled=True)]
    dot_general x260 -> x7, matrix products: 60.4 us -> 15.8 us  [the longest x1 5.11 us: body(): dzq_part = factor * jnp.dot(weights, zk, preferred_element_type=jnp.float32)]
  transfers between devices with their start and end apart: 193 -> 7, of which waited for: 193 -> 6; matrix products, arithmetic and copies ran while one was open for 3% -> 2% of each run, Pallas kernels for 0% -> 0%
where the time goes in v1:
time: 1000 us
  waiting for transfers between devices  831 us (83%)
  blocking collectives  118 us (12%)
  matrix products  19.7 us (2%)
  between operations  18 us (2%)
    psum x1, waiting for transfers between devices, body(): grad_head = lax.psum(head_part, BLK)  664 us
    psum x1, blocking collectives, body(): loss = lax.psum(loss_part, BLK + TP) / batch  74.4 us
    reduce_scatter x1, waiting for transfers between devices, body(): lax.psum_scatter(dzk_part, KG, scatter_dimension=0, tiled=True)  49.6 us
    all_gather x1, waiting for transfers between devices, body(): zk = lax.all_gather(zk_own, KG, axis=0, tiled=True)  48.9 us
    all_gather x1, waiting for transfers between devices, body(): zq = lax.all_gather(zq_own, QG, axis=0, tiled=True)  24.3 us
    reduce_scatter x1, waiting for transfers between devices, body(): lax.psum_scatter(zk_part, TP, scatter_dimension=0, tiled=True)  22.6 us
    reduce_scatter x1, waiting for transfers between devices, body(): lax.psum_scatter(zq_part, TP, scatter_dimension=0, tiled=True)  20.9 us
  transfers between devices with their start and end apart: 7, of which 6 were waited for; matrix products, arithmetic and copies ran while one was open for 2% of the time, Pallas kernels for 0%

profile of v1, /device:TPU:2, one launch (start us, length us, event | category | flops | bytes accessed | tf_op | source)
XLA Modules:
  0.0 1002.7 jit_solution(6069416242752123619)
XLA Ops:
  8.1 2.0 fusion.7
  10.1 1.9 fusion.8
  12.1 20.9 %reduce-scatter.5.cloned.1.call-done = f32[64,512]{1,0:T(8,128)} async-done(((f32[256,512]{1,0:T(8,128)}), f32[64,512]{1,0:T(8,128)}) %reduce-scatter.5.cloned.1.call-update) | async-done | bytes 131088 | tf_op jit(solution)/shard_map/reduce_scatter | solution.py:25
  33.0 1.5 convert_element_type.24
  34.7 22.6 %reduce-scatter.7.cloned.1.call-done = f32[64,512]{1,0:T(8,128)} async-done(((f32[256,512]{1,0:T(8,128)}), f32[64,512]{1,0:T(8,128)}) %reduce-scatter.7.cloned.1.call-update) | async-done | bytes 131088 | tf_op jit(solution)/shard_map/reduce_scatter | solution.py:26
  57.3 1.5 convert_element_type.25
  59.2 1.3 dynamic-slice
  62.0 14.1 %all-reduce = s32[1024]{0:T(1024)S(1)} all-reduce(s32[1024]{0:T(1024)S(1)} %dynamic-slice_dynamic-update-slice_fusion), channel_id=1, replica_groups=mesh['xlo'=2,'core'=2,'z'=8,'y'=4,'xh'=2] {'z','core'}, use_global_device_ids=true, to_apply=%add | all-reduce | flops 1024 | bytes 8192
  76.1 24.3 %all-gather.4.cloned.1.call-done = bf16[1024,512]{1,0:T(8,128)(2,1)} async-done(((bf16[64,512]{1,0:T(8,128)(2,1)}), bf16[1024,512]{1,0:T(8,128)(2,1)}) %all-gather.4.cloned.1.call-update) | async-done | bytes 1048592 | tf_op jit(solution)/shard_map/all_gather | solution.py:28
  100.4 48.9 %all-gather.6.cloned.1.call-done = bf16[1024,512]{1,0:T(8,128)(2,1)} async-done(((bf16[64,512]{1,0:T(8,128)(2,1)}), bf16[1024,512]{1,0:T(8,128)(2,1)}) %all-gather.6.cloned.1.call-update) | async-done | bytes 1048592 | tf_op jit(solution)/shard_map/all_gather | solution.py:29
  149.3 2.8 multiply_reduce_fusion
  152.1 1.9 copy-done.1
  154.0 3.4 fusion
  157.4 17.6 %all-gather = f32[16384]{0:T(1024)S(1)} all-gather(f32[1024]{0:T(1024)S(1)} %log_add_fusion.1), channel_id=2, replica_groups=mesh['xlo'=2,'core'=2,'z'=8,'y'=4,'xh'=2] {'z','core'}, dimensions={0}, use_global_device_ids=true | all-gather | bytes 69632 | tf_op jit(solution)/shard_map/all_gather | solution.py:48
  175.7 5.1 convolution_multiply_fusion.1
  180.9 4.9 convolution_multiply_fusion
  187.2 74.4 %psum.14 = f32[]{:T(128)} all-reduce(f32[]{:T(128)S(6)} %sub.34), channel_id=1, replica_groups=mesh['xlo'=2,'core'=2,'z'=8,'y'=4,'xh'=2] {'z','y','xh','xlo','core'}, use_global_device_ids=true, to_apply=%region_8.9 | all-reduce | flops 1 | bytes 8 | tf_op jit(solution)/shard_map/psum | solution.py:67
  262.3 0.9 convert_element_type.28
  263.2 5.9 all_gather.23
  269.1 49.6 %reduce-scatter.11.cloned.1.call-done = f32[64,512]{1,0:T(8,128)} async-done(((f32[1024,512]{1,0:T(8,128)}), f32[64,512]{1,0:T(8,128)}) %reduce-scatter.11.cloned.1.call-update) | async-done | bytes 131088 | tf_op jit(solution)/shard_map/reduce_scatter | solution.py:56
  319.7 5.8 all_gather.24
  325.7 1.0 fusion.3
  328.4 664.5 %all-reduce.3.cloned.1.call-done = f32[192,512]{1,0:T(8,128)} async-done(((f32[192,512]{1,0:T(8,128)}), f32[192,512]{1,0:T(8,128)}) %all-reduce.3.cloned.1.call-update) | async-done | bytes 393232 | tf_op jit(solution)/shard_map/psum | solution.py:66
  992.9 1.8 copy.10
  (44 shorter events, 6.1 us)
Async XLA Ops:
  7.2 0.9 copy-start
  7.2 25.9 %reduce-scatter.5.cloned.1.call-start = ((), (), s32[]{:S(2)}) async-start(), calls=%async_computation.4 | async-start | bytes 655360 | tf_op jit(solution)/shard_map/reduce_scatter | solution.py:25
  10.1 47.2 %reduce-scatter.7.cloned.1.call-start = ((), (), s32[]{:S(2)}) async-start(), calls=%async_computation.6 | async-start | bytes 655360 | tf_op jit(solution)/shard_map/reduce_scatter | solution.py:26
  12.1 88.3 %all-gather.4.cloned.1.call-start = ((), (), s32[]{:S(2)}) async-start(), calls=%async_computation.5 | async-start | bytes 1114112 | tf_op jit(solution)/shard_map/all_gather | solution.py:28
  34.6 114.7 %all-gather.6.cloned.1.call-start = ((), (), s32[]{:S(2)}) async-start(), calls=%async_computation.7 | async-start | bytes 1114112 | tf_op jit(solution)/shard_map/all_gather | solution.py:29
  58.8 203.5 %reduce-scatter.9.cloned.1.call-start = ((), (), s32[]{:S(2)}) async-start(), calls=%async_computation.8 | async-start | bytes 2228224 | tf_op jit(solution)/shard_map/reduce_scatter | solution.py:55
  152.1 1.9 copy-start.1
  152.1 23.6 %copy-start.5 = (bf16[1024,512]{1,0:T(8,128)(2,1)S(1)}, bf16[1024,512]{1,0:T(8,128)(2,1)}, u32[]{:S(2)}) copy-start(bf16[1024,512]{1,0:T(8,128)(2,1)} %all-gather.6.cloned.1.call-done) | copy-start | bytes 3145732
  175.7 5.2 copy-start.4
  180.8 144.6 %copy-start.3 = (bf16[256,192]{0,1:T(8,128)(2,1)S(1)}, bf16[256,192]{0,1:T(8,128)(2,1)}, u32[]{:S(2)}) copy-start(bf16[256,192]{0,1:T(8,128)(2,1)} %param.4) | copy-start | bytes 294916
  180.9 144.8 %copy-start.2 = (bf16[256,192]{0,1:T(8,128)(2,1)S(1)}, bf16[256,192]{0,1:T(8,128)(2,1)}, u32[]{:S(2)}) copy-start(bf16[256,192]{0,1:T(8,128)(2,1)} %param.5) | copy-start | bytes 294916
  180.9 137.9 %reduce-scatter.11.cloned.1.call-start = ((), (), s32[]{:S(2)}) async-start(), calls=%async_computation.9 | async-start | bytes 2228224 | tf_op jit(solution)/shard_map/reduce_scatter | solution.py:56
  185.8 807.1 %all-reduce.3.cloned.1.call-start = ((), (), s32[]{:S(2)}) async-start(), calls=%async_computation.10 | async-start | bytes 786432 | tf_op jit(solution)/shard_map/psum | solution.py:66
Sparse Core Ops, SparseCore 0:
  10.5 22.4 reduce-scatter.4
  35.6 21.6 reduce-scatter.6
  59.7 40.6 all-gather.3
  103.3 45.9 all-gather.5
  181.0 56.5 reduce-scatter.8
  241.0 77.7 reduce-scatter.10
  326.8 666.1 all-reduce.2

commit v2 on v1

v2 whole, which is shorter than its diff:
```python
import functools
import math

import jax
import jax.numpy as jnp
from jax import lax
from jax.experimental import pallas as pl
from jax.experimental.pallas import tpu as pltpu
from jax.sharding import Mesh, PartitionSpec as P

logit_gain = 3.0
TP = ("xlo", "core")
BLK = ("z", "y", "xh")
MESH = pl.DeviceIdType.MESH
F32 = jnp.float32
BF16 = jnp.bfloat16
NZ, NY, NX = 8, 4, 4
ROWS, OWN, EMB, FEAT = 256, 64, 512, 192
HALF = OWN // 2
BATCH = 16384
SCALE = logit_gain / math.sqrt(EMB)
N_SEMS = 144
NT = (((1,), (1,)), ((), ()))
TN = (((0,), (0,)), ((), ()))


def kernel(xq, xk, w, pair, loss_o, gq_o, gk_o, gh_o,
           fq, fk, wb, pbuf, zqa, zka, st, wt, lbuf,
           dqf, zs, zr, dk, ck, pk, k1, k2s, k2, dq4, dk4,
           gp, gs, g1r, g2r, g3r, l1, l2, l3, ss, rs):
    z, y, xh, xlo, c = [lax.axis_index(a) for a in ("z", "y", "xh", "xlo", "core")]
    x = 2 * xh + xlo
    t = 2 * xlo + c
    oc, oxlo, oxh = 1 - c, 1 - xlo, 1 - xh

    def at_z(d):
        return lax.rem(z + d, NZ)

    def at_y(d):
        return lax.rem(y + d, NY)

    def at_x(d):
        return lax.rem(x + d, NX)

    def dev_x(d):
        v = at_x(d)
        return {"xh": v // 2, "xlo": lax.rem(v, 2)}

    core_dev = {"core": oc}
    partner = {"xlo": oxlo}
    other = {"xlo": oxlo, "xh": oxh}
    cross = {"xlo": oxlo, "core": oc}
    z_dev = [{"z": at_z(d)} for d in range(NZ)]
    y_dev = [{"y": at_y(d)} for d in range(NY)]
    x_dev = [dev_x(d) for d in range(NX)]
    diag = [{"y": at_y(d), "xh": oxh} for d in range(NY)]

    peers = z_dev[1:] + y_dev[1:] + x_dev[1:] + diag[1:] + [core_dev, cross]
    barrier = pltpu.get_barrier_semaphore()
    for p in peers:
        pl.semaphore_signal(barrier, inc=1, device_id=p, device_id_type=MESH)
    pl.semaphore_wait(barrier, len(peers))

    copies = []

    def send(src, dst, dev):
        i = len(copies)
        cp = pltpu.make_async_remote_copy(src_ref=src, dst_ref=dst, send_sem=ss.at[i], recv_sem=rs.at[i],
                                          device_id=dev, device_id_type=MESH)
        cp.start()
        copies.append(cp)
        return cp

    def rows_of(a, b):
        return pl.ds((2 * a + b) * OWN, OWN)

    f2 = [send(r.at[rows_of(oxlo, c)], f.at[2], partner) for r, f in ((xq, fq), (xk, fk))]
    w2b = send(w.at[pl.ds(48, 144)], wb.at[2, pl.ds(48, 144)], other)
    f3 = [send(r.at[rows_of(oxlo, oc)], f.at[3], cross) for r, f in ((xq, fq), (xk, fk))]
    w2a = send(w.at[pl.ds(0, 48)], wb.at[2, pl.ds(0, 48)], partner)
    f1 = [send(r.at[rows_of(xlo, oc)], f.at[1], core_dev) for r, f in ((xq, fq), (xk, fk))]
    w1 = send(w, wb.at[1], core_dev)

    prow = pair[pl.ds(t, 1), :]
    pbuf[z] = jnp.concatenate([prow, prow], axis=1)
    pc = [send(pbuf.at[z], pbuf.at[z], z_dev[d]) for d in range(1, NZ)]

    own = rows_of(xlo, c)
    zq_acc = jnp.dot(xq[own, :], w[...], preferred_element_type=F32)
    zk_acc = jnp.dot(xk[own, :], w[...], preferred_element_type=F32)
    for cp in f1:
        cp.wait_recv()
    w1.wait_recv()
    zq_acc += jnp.dot(fq[1], wb[1], preferred_element_type=F32)
    zk_acc += jnp.dot(fk[1], wb[1], preferred_element_type=F32)
    w2a.wait_recv()
    w3a = send(wb.at[2, pl.ds(0, 48)], wb.at[3, pl.ds(0, 48)], core_dev)
    w2b.wait_recv()
    w3b = send(wb.at[2, pl.ds(48, 144)], wb.at[3, pl.ds(48, 144)], core_dev)
    for cp in f2:
        cp.wait_recv()
    zq_acc += jnp.dot(fq[2], wb[2], preferred_element_type=F32)
    zk_acc += jnp.dot(fk[2], wb[2], preferred_element_type=F32)
    for cp in f3:
        cp.wait_recv()
    w3a.wait_recv()
    w3b.wait_recv()
    zq_acc += jnp.dot(fq[3], wb[3], preferred_element_type=F32)
    zk_acc += jnp.dot(fk[3], wb[3], preferred_element_type=F32)
    zqa[z] = zq_acc.astype(BF16)
    zka[y, x, c] = zk_acc.astype(BF16)

    H = (pl.ds(0, HALF), pl.ds(HALF, HALF))
    up, down = z_dev[1], z_dev[NZ - 1]
    ring = {}
    for h in range(2):
        ring[0, 1, h] = send(zqa.at[z, H[h]], zqa.at[z, H[h]], up)
        ring[1, 1, h] = send(zqa.at[z, H[h]], zqa.at[z, H[h]], down)
    mine = zka.at[y, x, c]
    kx = [send(mine.at[H[0]], mine.at[H[0]], x_dev[d]) for d in range(1, NX)]
    ky = [send(mine.at[H[1]], mine.at[H[1]], y_dev[d]) for d in range(1, NY)]

    def ring_step(s):
        for h in range(2):
            for dr in range(2):
                if s == 5 or (s == 4 and h != dr):
                    continue
                ring[dr, s - 1, h].wait_recv()
                slab = at_z(NZ - s + 1) if dr == 0 else at_z(s - 1)
                ring[dr, s, h] = send(zqa.at[slab, H[h]], zqa.at[slab, H[h]], up if dr == 0 else down)

    ring_step(2)
    for cp in kx:
        cp.wait_recv()
    row0 = zka.at[y, :, c, H[0]]
    ky2 = [send(row0, row0, y_dev[d]) for d in range(1, NY)]
    for cp in ky:
        cp.wait_recv()
    col1 = zka.at[:, x, c, H[1]]
    kx2 = [send(col1, col1, x_dev[d]) for d in range(1, NX)]
    kc = [send(row0, row0, core_dev), send(col1, col1, core_dev)]
    ring_step(3)
    ring_step(4)
    for d in range(1, NY):
        ky2[d - 1].wait_recv()
        r = zka.at[at_y(NY - d), :, c, H[0]]
        kc.append(send(r, r, core_dev))
    for d in range(1, NX):
        kx2[d - 1].wait_recv()
        r = zka.at[:, at_x(NX - d), c, H[1]]
        kc.append(send(r, r, core_dev))
    for h in range(2):
        for dr in range(2):
            if h != dr:
                ring[dr, 3, h].wait_recv()
            else:
                ring[dr, 4, h].wait_recv()
    for cp in kc:
        cp.wait_recv()
    for cp in pc:
        cp.wait_recv()

    zq = zqa[...].reshape(NZ * OWN, EMB)

    def score_step(i, top):
        keys = zka[i // 2, pl.ds(lax.rem(i, 2) * 2, 2)].reshape(256, EMB)
        s = SCALE * lax.dot_general(keys, zq, NT, preferred_element_type=F32)
        st[i] = s
        return jnp.maximum(top, jnp.max(s, axis=0, keepdims=True))

    top = lax.fori_loop(0, 8, score_step, jnp.full((1, 512), -1e30, F32))

    def sum_step(i, total):
        return total + jnp.sum(jnp.exp(st[i] - top), axis=0, keepdims=True)

    total = lax.fori_loop(0, 8, sum_step, jnp.zeros((1, 512), F32))
    lbuf[z] = top + jnp.log(total)
    lc = [send(lbuf.at[z], lbuf.at[z], z_dev[d]) for d in range(1, NZ)]
    lane = lax.broadcasted_iota(jnp.int32, (1, 128), 1)
    pairs = jnp.concatenate([jnp.where(lane < 64, pbuf[2 * j], pbuf[2 * j + 1]) for j in range(4)], axis=1)
    pairs = pairs - z * 2048
    for cp in lc:
        cp.wait_recv()
    parts = [lbuf[i] for i in range(NZ)]
    lse_top = functools.reduce(jnp.maximum, parts)
    lse = lse_top + jnp.log(functools.reduce(jnp.add, [jnp.exp(p - lse_top) for p in parts]))

    key_iota = lax.broadcasted_iota(jnp.int32, (256, 512), 0)
    dqf[...] = jnp.zeros_like(dqf)

    def weight_step(i, pos):
        s = st[i]
        hit = (key_iota + i * 256) == pairs
        e = jnp.exp(s - lse)
        wt[i] = jnp.where(hit, e - 1.0, e).astype(BF16)
        keys = zka[i // 2, pl.ds(lax.rem(i, 2) * 2, 2)].reshape(256, EMB)
        dqf[...] += lax.dot_general(wt[i], keys, TN, preferred_element_type=F32).reshape(NZ, OWN, EMB)
        return pos + jnp.sum(jnp.where(hit, s, 0.0), axis=0, keepdims=True)

    pos = lax.fori_loop(0, 8, weight_step, jnp.zeros((1, 512), F32))
    lane5 = lax.broadcasted_iota(jnp.int32, (1, 512), 1)
    loss_row = jnp.where((lane5 >= z * OWN) & (lane5 < z * OWN + OWN), lse, 0.0) - pos
    loss_row = loss_row[:, 0:128] + loss_row[:, 128:256] + loss_row[:, 256:384] + loss_row[:, 384:512]

    FAC = SCALE / BATCH
    rz = {}

    def zred_step(s):
        for h in range(2):
            for dr in range(2):
                if s == 1 and h != dr:
                    continue
                dest = at_z(5 - s) if dr == 0 else at_z(NZ - 5 + s)
                v = dqf[dest, H[h], :] * FAC
                if s >= 3 or (s == 2 and h == dr):
                    rz[dr, s - 1, h].wait_recv()
                    v += zr[dr, s - 2, H[h], :].astype(F32)
                zs[dr, s - 1, H[h], :] = v.astype(BF16)
                rz[dr, s, h] = send(zs.at[dr, s - 1, H[h]], zr.at[dr, s - 1, H[h]], up if dr == 0 else down)

    zred_step(1)

    kcs = []
    for d in (1, 2, 3, 0):
        yy = at_y(d)

        def key_step(j, carry, yy=yy):
            g = jnp.dot(wt[yy * 2 + j], zq, preferred_element_type=F32) * FAC
            dk[yy, pl.ds(j * 2, 2)] = g.astype(BF16).reshape(2, 2, OWN, EMB)
            return carry

        lax.fori_loop(0, 2, key_step, 0)
        kcs.append((yy, send(dk.at[yy, :, oc], ck.at[yy], core_dev)))
        if d == 2:
            zred_step(2)
    for yy, cp in kcs:
        cp.wait_recv()
        pk[yy] = (dk[yy, :, c].astype(F32) + ck[yy].astype(F32)).astype(BF16)
    a1 = [send(pk.at[at_y(d), :, H[0]], k1.at[0, y], y_dev[d]) for d in range(1, NY)]
    b1 = [send(pk.at[:, at_x(d), H[1]], k1.at[1, x], x_dev[d]) for d in range(1, NX)]
    zred_step(3)
    zred_step(4)
    k1[0, y] = pk[y, :, H[0], :]
    k1[1, x] = pk[:, x, H[1], :]
    for cp in a1:
        cp.wait_recv()
    k2s[0] = functools.reduce(jnp.add, [k1[0, i].astype(F32) for i in range(4)]).astype(BF16)
    a2 = [send(k2s.at[0, at_x(d)], k2.at[0, x], x_dev[d]) for d in range(1, NX)]
    for cp in b1:
        cp.wait_recv()
    k2s[1] = functools.reduce(jnp.add, [k1[1, i].astype(F32) for i in range(4)]).astype(BF16)
    b2 = [send(k2s.at[1, at_y(d)], k2.at[1, y], y_dev[d]) for d in range(1, NY)]
    k2[0, x] = k2s[0, x]
    k2[1, y] = k2s[1, y]
    v = dqf[z] * FAC
    for dr in range(2):
        for h in range(2):
            rz[dr, 4, h].wait_recv()
        v += zr[dr, 3].astype(F32)
    dq4[t] = v.astype(BF16)
    l1[t] = loss_row
    tpt = 2 * oxlo + c
    q1 = send(dq4.at[t], dq4.at[t], partner)
    q2 = send(dq4.at[t], dq4.at[t], core_dev)
    lo1 = [send(l1.at[t], l1.at[t], p) for p in (core_dev, partner, cross)]
    for cp in a2 + b2:
        cp.wait_recv()
    for h in range(2):
        dk4[t, H[h], :] = functools.reduce(jnp.add, [k2[h, i].astype(F32) for i in range(4)]).astype(BF16)
    d1 = send(dk4.at[t], dk4.at[t], partner)
    d2 = send(dk4.at[t], dk4.at[t], core_dev)
    q1.wait_recv()
    q3 = send(dq4.at[tpt], dq4.at[tpt], core_dev)
    d1.wait_recv()
    d3 = send(dk4.at[tpt], dk4.at[tpt], core_dev)
    for cp in (q2, q3):
        cp.wait_recv()
    dq = dq4[...].reshape(ROWS, EMB)
    head = lax.dot_general(xq[...], dq, TN, preferred_element_type=F32)
    for cp in (d2, d3):
        cp.wait_recv()
    dkv = dk4[...].reshape(ROWS, EMB)
    head += lax.dot_general(xk[...], dkv, TN, preferred_element_type=F32)

    for i in range(4):
        for j in range(2):
            piece = head[i * 48:(i + 1) * 48, j * 256:(j + 1) * 256]
            gp[i, j] = piece
            gs[i, j] = piece.astype(BF16)
    for cp in lo1:
        cp.wait_recv()
    l2[y, xh] = l1[0] + l1[1] + l1[2] + l1[3]
    plane = [(y_dev[d], at_y(d), xh) for d in range(1, NY)] + [({"xh": oxh}, y, oxh)] + [
        (diag[d], at_y(d), oxh) for d in range(1, NY)]
    h1 = [send(gs.at[py, px], g1r.at[y, xh], p) for p, py, px in plane]
    lo2 = [send(l2.at[y, xh], l2.at[y, xh], p) for p, py, px in plane]
    gq_o[...] = lax.dot_general(dq, w[...], NT, preferred_element_type=F32).astype(BF16)
    gk_o[...] = lax.dot_general(dkv, w[...], NT, preferred_element_type=F32).astype(BF16)
    g1r[y, xh] = gs[y, xh]
    for cp in h1 + lo2:
        cp.wait_recv()
    order = [(i, j) for i in range(4) for j in range(2)]
    g2r[z] = functools.reduce(jnp.add, [g1r[i, j].astype(F32) for i, j in order]).astype(BF16)
    l3[z] = functools.reduce(jnp.add, [l2[i, j] for i, j in order])
    h2 = [send(g2r.at[z], g2r.at[z], z_dev[d]) for d in range(1, NZ)]
    lo3 = [send(l3.at[z], l3.at[z], z_dev[d]) for d in range(1, NZ)]
    for cp in h2 + lo3:
        cp.wait_recv()
    g3r[y, xh] = functools.reduce(jnp.add, [g2r[i].astype(F32) for i in range(NZ)])
    h3 = [send(g3r.at[y, xh], g3r.at[y, xh], p) for p, py, px in plane]
    row = functools.reduce(jnp.add, [l3[i] for i in range(NZ)])
    loss_o[...] = jnp.broadcast_to(jnp.sum(row, axis=1, keepdims=True) / BATCH, (1, 128))
    for cp in h3:
        cp.wait_recv()
    for i, j in order:
        gh_o[i * 48:(i + 1) * 48, j * 256:(j + 1) * 256] = g3r[i, j]
    for cp in copies:
        cp.wait_send()


def body(query_feat, key_feat, head_weight, pair):
    vmem = pl.BlockSpec(memory_space=pltpu.VMEM)
    V = pltpu.VMEM
    loss, gq, gk, gh = pl.pallas_call(
        kernel,
        out_shape=(
            jax.ShapeDtypeStruct((1, 128), F32),
            jax.ShapeDtypeStruct((ROWS, FEAT), BF16),
            jax.ShapeDtypeStruct((ROWS, FEAT), BF16),
            jax.ShapeDtypeStruct((FEAT, EMB), F32),
        ),
        in_specs=[vmem] * 4,
        out_specs=(vmem,) * 4,
        scratch_shapes=[
            V((4, OWN, FEAT), BF16), V((4, OWN, FEAT), BF16), V((4, FEAT, EMB), BF16),
            V((NZ, 1, 128), jnp.int32),
            V((NZ, OWN, EMB), BF16), V((NY, NX, 2, OWN, EMB), BF16),
            V((8, 256, 512), F32), V((8, 256, 512), BF16),
            V((NZ, 1, 512), F32),
            V((NZ, OWN, EMB), F32), V((2, 4, OWN, EMB), BF16), V((2, 4, OWN, EMB), BF16),
            V((NY, NX, 2, OWN, EMB), BF16), V((NY, NX, OWN, EMB), BF16), V((NY, NX, OWN, EMB), BF16),
            V((2, 4, 4, HALF, EMB), BF16), V((2, 4, HALF, EMB), BF16), V((2, 4, HALF, EMB), BF16),
            V((4, OWN, EMB), BF16), V((4, OWN, EMB), BF16),
            V((4, 2, 48, 256), F32), V((4, 2, 48, 256), BF16), V((4, 2, 48, 256), BF16),
            V((NZ, 48, 256), BF16), V((4, 2, 48, 256), F32),
            V((4, 1, 128), F32), V((4, 2, 1, 128), F32), V((NZ, 1, 128), F32),
            pltpu.SemaphoreType.DMA((N_SEMS,)), pltpu.SemaphoreType.DMA((N_SEMS,)),
        ],
        compiler_params=pltpu.CompilerParams(collective_id=0, has_side_effects=True, vmem_limit_bytes=48 << 20),
    )(query_feat, key_feat, head_weight, pair.reshape(4, OWN))
    return loss[0, 0], gq, gk, gh


def solution(mesh):
    shape = {"tp": (2, 2), "blk": (8, 4, 2)}
    names = {"tp": TP, "blk": BLK}
    a, b = mesh.axis_names
    fine = Mesh(mesh.devices.reshape(shape[a] + shape[b]), names[a] + names[b])
    in_specs = (P(BLK, TP), P(BLK, TP), P(TP, None), P(BLK))
    out_specs = (P(), P(BLK, TP), P(BLK, TP), P(TP, None))
    return jax.shard_map(body, mesh=fine, in_specs=in_specs, out_specs=out_specs, check_vma=False)
```

time: 1000 us -> 92.3 us (0.09)
  waiting for transfers between devices: 831 us -> 0 us
  blocking collectives: 118 us -> 0 us
  Pallas kernels: 0 us -> 86.1 us
  matrix products: 19.7 us -> 0 us
  between operations: 18 us -> 1.85 us
    psum x1 -> x0, waiting for transfers between devices: 664 us -> none  [body(): grad_head = lax.psum(head_part, BLK)]
    reduce_scatter x4 -> x0, waiting for transfers between devices: 93.2 us -> none  [the longest x1 49.6 us: body(): lax.psum_scatter(dzk_part, KG, scatter_dimension=0, tiled=True)]
    pallas_call x0 -> x1, Pallas kernels: none -> 86.1 us  [body(): pl.pallas_call(kernel, out_shape=(jax.ShapeDtypeStruct((1, 128), F32), ja...]
    psum x1 -> x0, blocking collectives: 74.4 us -> none  [body(): loss = lax.psum(loss_part, BLK + TP) / batch]
    all_gather x2 -> x0, waiting for transfers between devices: 73.2 us -> none  [the longest x1 48.9 us: body(): zk = lax.all_gather(zk_own, KG, axis=0, tiled=True)]
    all_gather x3 -> x0, blocking collectives: 29.2 us -> none  [the longest x1 17.6 us: body(): lse_parts = lax.all_gather(lse_part, QG, axis=0)]
    dot_general x9 -> x0, matrix products: 19.7 us -> none  [the longest x1 5.11 us: body(): dzq_part = factor * jnp.dot(weights, zk, preferred_element_type=jnp.float32)]
    unnamed x1 -> x0, blocking collectives: 14.1 us -> none
  transfers between devices with their start and end apart: 7 -> 0, of which waited for: 6 -> 0; matrix products, arithmetic and copies ran while one was open for 2% -> 0% of each run, Pallas kernels for 0% -> 0%
where the time goes in v2:
time: 92.3 us; the launch traced here: 92.1 us
  Pallas kernels  86.1 us (93%)
  local copies, waits for them, and re-layouts  4.17 us (5%)
  between operations  1.85 us (2%)
    pallas_call x1, Pallas kernels, body(): pl.pallas_call(kernel, out_shape=(jax.ShapeDtypeStruct((1, 128), F32), ja...  86.1 us
    unnamed x9, local copies, waits for them, and re-layouts  3.37 us

profile of v2, /device:TPU:2, one launch (start us, length us, event | category | flops | bytes accessed | tf_op | source)
XLA Modules:
  0.0 92.1 jit_solution(12759517525701220719)
XLA Ops:
  0.6 0.0 copy-start.1
  0.6 0.8 reshape.11.pair
  1.4 0.0 copy-start
  1.4 1.0 %copy.8.xq = bf16[256,192]{1,0:T(8,128)(2,1)S(1)} copy(bf16[256,192]{0,1:T(8,128)(2,1)} %param.4) | data formatting | bytes 196608 | tf_op args[0]
  2.5 0.0 copy-done.1
  2.5 0.1 copy.9.xk
  2.6 0.0 copy-done
  2.6 86.1 %shard_map.75 = (f32[1,128]{1,0:T(1,128)S(1)}, bf16[256,192]{1,0:T(8,128)(2,1)S(1)}, bf16[256,192]{1,0:T(8,128)(2,1)S(1)}, f32[192,512]{1,0:T(8,128)S(1)}) custom-call(bf16[256,192]{1,0:T(8,128)(2,1)S(1)} %copy.8.xq, bf16[256,192]{1,0:T(8,128)(2,1)S(1)} %copy.9.xk, bf16[192,512]{1,0:T(8,128)(2,1)S(1)} %copy-done, s32[4,64]{1,0:T(4,128)S(1)} %reshape.11.pair), custom_call_target="tpu_custom_call" | custom-call | tf_op jit(solution)/shard_map/pallas_call | solution.py:324
  88.7 0.7 copy.10
  89.5 0.7 copy.11
  90.3 0.7 copy.15
Async XLA Ops:
  0.6 1.8 %copy-start.1 = (bf16[256,192]{0,1:T(8,128)(2,1)S(1)}, bf16[256,192]{0,1:T(8,128)(2,1)}, u32[]{:S(2)}) copy-start(bf16[256,192]{0,1:T(8,128)(2,1)} %param.5) | copy-start | bytes 294916
  1.4 1.2 %copy-start = (bf16[192,512]{1,0:T(8,128)(2,1)S(1)}, bf16[192,512]{1,0:T(8,128)(2,1)}, u32[]{:S(2)}) copy-start(bf16[192,512]{1,0:T(8,128)(2,1)} %w.1) | copy-start | bytes 589828

commit v3 on v2

v3 whole, which is shorter than its diff:
```python
import functools
import math

import jax
import jax.numpy as jnp
from jax import lax
from jax.experimental import pallas as pl
from jax.experimental.pallas import tpu as pltpu
from jax.sharding import Mesh, PartitionSpec as P

logit_gain = 3.0
TP = ("xlo", "core")
BLK = ("z", "y", "xh")
MESH = pl.DeviceIdType.MESH
F32 = jnp.float32
BF16 = jnp.bfloat16
NZ, NY, NX = 8, 4, 4
ROWS, OWN, EMB, FEAT = 256, 64, 512, 192
HALF = OWN // 2
BATCH = 16384
SCALE = logit_gain / math.sqrt(EMB)
N_SEMS = 192
NT = (((1,), (1,)), ((), ()))
TN = (((0,), (0,)), ((), ()))


OFF = (0, 1, 7, 2, 6, 3, 5, 4)
SLOT = {o: k for k, o in enumerate(OFF)}
FAR = (4, 3, 5, 2, 6, 1, 7)


def add_all(values):
    return functools.reduce(jnp.add, values)


def kernel(xq_h, xk_h, w_h, pair_h, loss_o, gq_h, gk_h, gh_o,
           xqt, xkt, xq, xk, w, pair, gq_v, gk_v, f, wb, pbuf, zqa, zka, st, wt, lbuf, lsum,
           dqf, zs, zr, dk, ck, pk, k1, k2s, k2, dq4, dk4,
           gs, g1r, g2r, g3s, g3r, l1, l2, l3, ss, rs, ls):
    z, y, xh, xlo, c = [lax.axis_index(a) for a in ("z", "y", "xh", "xlo", "core")]
    x = 2 * xh + xlo
    t = 2 * xlo + c
    oc, oxlo, oxh = 1 - c, 1 - xlo, 1 - xh

    loads = [pltpu.make_async_copy(a, b, ls.at[i]) for i, (a, b) in enumerate(
        ((xq_h, xqt), (xk_h, xkt), (w_h, w), (pair_h, pair)))]
    for cp in loads:
        cp.start()

    def at_z(d):
        return lax.rem(z + d, NZ)

    def at_y(d):
        return lax.rem(y + d, NY)

    def at_x(d):
        return lax.rem(x + d, NX)

    def dev_x(d):
        v = at_x(d)
        return {"xh": v // 2, "xlo": lax.rem(v, 2)}

    core_dev = {"core": oc}
    partner = {"xlo": oxlo}
    other = {"xlo": oxlo, "xh": oxh}
    cross = {"xlo": oxlo, "core": oc}
    z_dev = [{"z": at_z(d)} for d in range(NZ)]
    y_dev = [{"y": at_y(d)} for d in range(NY)]
    x_dev = [dev_x(d) for d in range(NX)]
    diag = [{"y": at_y(d), "xh": oxh} for d in range(NY)]

    peers = [z_dev[1], z_dev[7]] + y_dev[1:] + x_dev[1:] + [core_dev, cross]
    barrier = pltpu.get_barrier_semaphore()
    for p in peers:
        pl.semaphore_signal(barrier, inc=1, device_id=p, device_id_type=MESH)
    for cp in loads:
        cp.wait()
    xq[...] = xqt[...].T
    xk[...] = xkt[...].T
    pl.semaphore_wait(barrier, len(peers))

    copies = []

    def send(src, dst, dev):
        i = len(copies)
        cp = pltpu.make_async_remote_copy(src_ref=src, dst_ref=dst, send_sem=ss.at[i], recv_sem=rs.at[i],
                                          device_id=dev, device_id_type=MESH)
        cp.start()
        copies.append(cp)
        return cp

    def rows_of(a, b):
        return pl.ds((2 * a + b) * OWN, OWN)

    feats = ((xq, 0), (xk, 1))
    W = [pl.ds(48 * i, 48) for i in range(4)]
    f2 = [send(r.at[rows_of(oxlo, c)], f.at[2, i], partner) for r, i in feats]
    w2 = {i: send(w.at[W[i]], wb.at[2, W[i]], other) for i in (1, 2, 3)}
    f3 = [send(r.at[rows_of(oxlo, oc)], f.at[3, i], cross) for r, i in feats]
    w2[0] = send(w.at[W[0]], wb.at[2, W[0]], partner)
    f1 = [send(r.at[rows_of(xlo, oc)], f.at[1, i], core_dev) for r, i in feats]
    w1 = send(w, wb.at[1], core_dev)

    own = rows_of(xlo, c)

    def project(rows, weights):
        return jnp.dot(rows, weights, preferred_element_type=F32)

    acc = project(jnp.concatenate([xq[own, :], xk[own, :]], axis=0), w[...])
    for cp in f1:
        cp.wait_recv()
    w1.wait_recv()
    acc += project(f[1].reshape(2 * OWN, FEAT), wb[1])
    w3 = []
    for i in (1, 2, 0, 3):
        w2[i].wait_recv()
        w3.append(send(wb.at[2, W[i]], wb.at[3, W[i]], core_dev))
    for cp in f2:
        cp.wait_recv()
    acc += project(f[2].reshape(2 * OWN, FEAT), wb[2])
    for cp in f3 + w3:
        cp.wait_recv()
    acc += project(f[3].reshape(2 * OWN, FEAT), wb[3])
    zqa[0] = acc[:OWN].astype(BF16)
    zka[y, x, c] = acc[OWN:].astype(BF16)

    H = (pl.ds(0, HALF), pl.ds(HALF, HALF))
    ALL = pl.ds(0, OWN)
    up, down = z_dev[1], z_dev[NZ - 1]
    mine = zka.at[y, x, c]

    def ring_send(s, part=ALL):
        a, b = SLOT[(NZ - s + 1) % NZ], SLOT[s - 1]
        a2, b2 = SLOT[NZ - s], SLOT[s]
        pa, pb = (H[0], H[1]) if s == 4 else (ALL, ALL)
        return (send(zqa.at[a, pa], zqa.at[a2, pa], up), send(zqa.at[b, pb], zqa.at[b2, pb], down))

    NEAR = (2, 1, 3)
    r1 = ring_send(1)
    kx = {d: send(mine.at[H[0]], mine.at[H[0]], x_dev[d]) for d in NEAR}
    ky = {d: send(mine.at[H[1]], mine.at[H[1]], y_dev[d]) for d in NEAR}
    ky2 = {d: [] for d in NEAR}
    kx2 = {d: [] for d in NEAR}

    def spread_y(r):
        for d in NEAR:
            ky2[d].append(send(r, r, y_dev[d]))

    def spread_x(r):
        for d in NEAR:
            kx2[d].append(send(r, r, x_dev[d]))

    spread_y(mine.at[H[0]])
    spread_x(mine.at[H[1]])
    for cp in r1:
        cp.wait_recv()
    r2 = ring_send(2)
    for d in (1, 3, 2):
        kx[d].wait_recv()
        spread_y(zka.at[y, at_x(NX - d), c, H[0]])
        ky[d].wait_recv()
        spread_x(zka.at[at_y(NY - d), x, c, H[1]])
    row0 = zka.at[y, :, c, H[0]]
    col1 = zka.at[:, x, c, H[1]]
    kc = [send(row0, row0, core_dev), send(col1, col1, core_dev)]
    for cp in r2:
        cp.wait_recv()
    r3 = ring_send(3)
    for d in (1, 3):
        for cp in ky2[d]:
            cp.wait_recv()
        r = zka.at[at_y(NY - d), :, c, H[0]]
        kc.append(send(r, r, core_dev))
        for cp in kx2[d]:
            cp.wait_recv()
        r = zka.at[:, at_x(NX - d), c, H[1]]
        kc.append(send(r, r, core_dev))
    for cp in r3:
        cp.wait_recv()
    r4 = ring_send(4)
    for cp in ky2[2]:
        cp.wait_recv()
    r = zka.at[at_y(2), :, c, H[0]]
    kc.append(send(r, r, core_dev))
    for cp in kx2[2]:
        cp.wait_recv()
    r = zka.at[:, at_x(2), c, H[1]]
    kc.append(send(r, r, core_dev))
    for cp in kc:
        cp.wait_recv()

    def keys_at(i):
        return zka[i // 2, pl.ds(lax.rem(i, 2) * 2, 2)].reshape(256, EMB)

    def scores_of(g):
        q = zqa[pl.ds(4 * g, 4)].reshape(256, EMB)

        def score_step(i, top):
            s = SCALE * lax.dot_general(keys_at(i), q, NT, preferred_element_type=F32)
            st[g, i] = s
            return jnp.maximum(top, jnp.max(s, axis=0, keepdims=True))

        top = lax.fori_loop(0, 8, score_step, jnp.full((1, 256), -1e30, F32))

        def sum_step(i, total):
            return total + jnp.sum(jnp.exp(st[g, i] - top), axis=0, keepdims=True)

        return top + jnp.log(lax.fori_loop(0, 8, sum_step, jnp.zeros((1, 256), F32)))

    lane = lax.broadcasted_iota(jnp.int32, (1, 128), 1)
    low = lane < OWN

    def put_parts(g, row):
        for j in range(2):
            v = row[:, 128 * j:128 * j + 128]
            turned = pltpu.roll(v, OWN, 1)
            lbuf[z, at_z(OFF[4 * g + 2 * j])] = jnp.where(low, v, turned)
            lbuf[z, at_z(OFF[4 * g + 2 * j + 1])] = jnp.where(low, turned, v)

    put_parts(0, scores_of(0))
    for cp in r4:
        cp.wait_recv()
    put_parts(1, scores_of(1))
    lc = [send(lbuf.at[z], lbuf.at[z], z_dev[d]) for d in FAR]
    prow = pair[pl.ds(xlo, 1), :]
    pbuf[z] = jnp.where((lane // OWN) == c, prow, pltpu.roll(prow, OWN, 1))
    pc = [send(pbuf.at[z], pbuf.at[z], z_dev[d]) for d in FAR]
    key_iota = lax.broadcasted_iota(jnp.int32, (256, 256), 0)
    for cp in lc + pc:
        cp.wait_recv()
    for i in range(NZ):
        parts = [lbuf[k, i] for k in range(NZ)]
        m = functools.reduce(jnp.maximum, parts)
        lsum[i] = m + jnp.log(add_all([jnp.exp(p - m) for p in parts]))

    def in_order(at):
        return [jnp.concatenate([jnp.where(low, at(at_z(OFF[4 * g + 2 * j])), at(at_z(OFF[4 * g + 2 * j + 1])))
                                 for j in range(2)], axis=1) for g in range(2)]

    lse = in_order(lambda i: lsum[i])
    pairs = [p - z * 2048 for p in in_order(lambda i: pbuf[i])]

    FAC = SCALE / BATCH
    zq = zqa[...].reshape(NZ * OWN, EMB)
    a1, b1 = [], []

    def key_rows(yy, pos):
        def step(j, pos):
            i = yy * 2 + j
            new = []
            for g in range(2):
                s = st[g, i]
                hit = (key_iota + i * 256) == pairs[g]
                e = jnp.exp(s - lse[g])
                wt[i, :, 256 * g:256 * g + 256] = jnp.where(hit, e - 1.0, e).astype(BF16)
                new.append(pos[g] + jnp.sum(jnp.where(hit, s, 0.0), axis=0, keepdims=True))
            v = jnp.dot(wt[i], zq, preferred_element_type=F32) * FAC
            dk[yy, pl.ds(j * 2, 2)] = v.astype(BF16).reshape(2, 2, OWN, EMB)
            return tuple(new)

        return lax.fori_loop(0, 2, step, pos), send(dk.at[yy, :, oc], ck.at[yy], core_dev)

    def core_sum(d, cp):
        yy = at_y(d)
        cp.wait_recv()
        pk[yy] = (dk[yy, :, c].astype(F32) + ck[yy].astype(F32)).astype(BF16)
        if d:
            a1.append(send(pk.at[yy, :, H[0]], k1.at[0, y], y_dev[d]))
        for e in NEAR:
            b1.append(send(pk.at[yy, at_x(e), H[1]], k1.at[1, x, yy], x_dev[e]))

    pos = (jnp.zeros((1, 256), F32),) * 2
    pos, c2 = key_rows(at_y(2), pos)
    pos, c1 = key_rows(at_y(1), pos)
    core_sum(2, c2)
    pos, c3 = key_rows(at_y(3), pos)
    core_sum(1, c1)
    pos, c0 = key_rows(at_y(0), pos)
    core_sum(3, c3)

    def query_rows(g):
        wg = wt[:, :, 256 * g:256 * g + 256].reshape(2048, 256)
        v = lax.dot_general(wg, zka[...].reshape(2048, EMB), TN, preferred_element_type=F32) * FAC
        dqf[pl.ds(4 * g, 4)] = v.reshape(4, OWN, EMB)

    query_rows(1)
    def ahead(dr, d):
        return d if dr == 0 else NZ - d

    zc = {}
    for dr in range(2):
        zs[dr, 1, H[dr], :] = dqf[SLOT[4], H[dr], :].astype(BF16)
        zc[dr, 1] = send(zs.at[dr, 1, H[dr]], zr.at[dr, 1, H[dr]], z_dev[ahead(dr, 2)])
        zs[dr, 0] = dqf[SLOT[ahead(dr, 3)]].astype(BF16)
        zc[dr, 0] = send(zs.at[dr, 0], zr.at[dr, 0], z_dev[ahead(dr, 1)])
    core_sum(0, c0)
    k1[0, y] = pk[y, :, H[0], :]
    k1[1, x] = pk[:, x, H[1], :]
    query_rows(0)
    for dr in range(2):
        zs[dr, 2] = dqf[SLOT[ahead(dr, 1)]].astype(BF16)
        zc[dr, 2] = send(zs.at[dr, 2], zr.at[dr, 2], z_dev[ahead(dr, 1)])
    lanes0 = jnp.where(low, lse[0][:, :128], 0.0)
    l1[t] = lanes0 - add_all([p[:, 128 * j:128 * j + 128] for p in pos for j in range(2)])
    lo1 = [send(l1.at[t], l1.at[t], p) for p in (core_dev, partner, cross)]
    for dr in range(2):
        v = dqf[SLOT[ahead(dr, 2)]]
        zc[dr, 0].wait_recv()
        v += zr[dr, 0].astype(F32)
        zc[dr, 1].wait_recv()
        pieces = [v[:HALF], v[HALF:]]
        pieces[dr] += zr[dr, 1, H[dr], :].astype(F32)
        for h in range(2):
            zs[dr, 3, H[h], :] = pieces[h].astype(BF16)
        zc[dr, 3] = send(zs.at[dr, 3], zr.at[dr, 3], z_dev[ahead(dr, 2)])
    for cp in a1:
        cp.wait_recv()
    k2s[0] = add_all([k1[0, i].astype(F32) for i in range(4)]).astype(BF16)
    a2 = [send(k2s.at[0, at_x(d)], k2.at[0, x], x_dev[d]) for d in NEAR]
    for cp in b1:
        cp.wait_recv()
    k2s[1] = add_all([k1[1, i].astype(F32) for i in range(4)]).astype(BF16)
    b2 = [send(k2s.at[1, at_y(d)], k2.at[1, y], y_dev[d]) for d in NEAR]
    k2[0, x] = k2s[0, x]
    k2[1, y] = k2s[1, y]
    v = dqf[0]
    for dr in range(2):
        for i in (2, 3):
            zc[dr, i].wait_recv()
            v += zr[dr, i].astype(F32)
    dq4[t] = v.astype(BF16)
    tpt = 2 * oxlo + c
    q1 = send(dq4.at[t], dq4.at[t], partner)
    q2 = send(dq4.at[t], dq4.at[t], core_dev)
    for cp in a2 + b2:
        cp.wait_recv()
    for h in range(2):
        dk4[t, H[h], :] = add_all([k2[h, i].astype(F32) for i in range(4)]).astype(BF16)
    d1 = send(dk4.at[t], dk4.at[t], partner)
    d2 = send(dk4.at[t], dk4.at[t], core_dev)
    q1.wait_recv()
    q3 = send(dq4.at[tpt], dq4.at[tpt], core_dev)
    d1.wait_recv()
    d3 = send(dk4.at[tpt], dk4.at[tpt], core_dev)
    for cp in (q2, q3):
        cp.wait_recv()
    dq = dq4[...].reshape(ROWS, EMB)
    head = jnp.dot(xqt[...], dq, preferred_element_type=F32)
    for cp in (d2, d3):
        cp.wait_recv()
    dkv = dk4[...].reshape(ROWS, EMB)
    head += jnp.dot(xkt[...], dkv, preferred_element_type=F32)

    for i in range(4):
        for j in range(2):
            gs[i, j] = head[i * 48:(i + 1) * 48, j * 256:(j + 1) * 256].astype(BF16)
    plane = [(diag[2], at_y(2), oxh), (diag[1], at_y(1), oxh), (diag[3], at_y(3), oxh), (y_dev[2], at_y(2), xh),
             ({"xh": oxh}, y, oxh), (y_dev[1], at_y(1), xh), (y_dev[3], at_y(3), xh)]
    h1 = [send(gs.at[py, px], g1r.at[y, xh], p) for p, py, px in plane]
    for cp in lo1:
        cp.wait_recv()
    l2[y, xh] = l1[0] + l1[1] + l1[2] + l1[3]
    lo2 = [send(l2.at[y, xh], l2.at[y, xh], p) for p, py, px in plane]
    gq_v[...] = lax.dot_general(w[...], dq, NT, preferred_element_type=F32).astype(BF16)
    gk_v[...] = lax.dot_general(w[...], dkv, NT, preferred_element_type=F32).astype(BF16)
    stores = [pltpu.make_async_copy(a, b, ls.at[i]) for i, (a, b) in enumerate(((gq_v, gq_h), (gk_v, gk_h)))]
    for cp in stores:
        cp.start()
    g1r[y, xh] = gs[y, xh]
    for cp in h1:
        cp.wait_recv()
    order = [(i, j) for i in range(4) for j in range(2)]
    g2r[z] = add_all([g1r[i, j].astype(F32) for i, j in order]).astype(BF16)
    h2 = [send(g2r.at[z], g2r.at[z], z_dev[d]) for d in FAR]
    for cp in lo2:
        cp.wait_recv()
    l3[z] = add_all([l2[i, j] for i, j in order])
    lo3 = [send(l3.at[z], l3.at[z], z_dev[d]) for d in FAR]
    for cp in h2:
        cp.wait_recv()
    g3s[...] = add_all([g2r[i].astype(F32) for i in range(NZ)]).astype(BF16)
    g3r[y, xh] = g3s[...]
    h3 = [send(g3s, g3r.at[y, xh], p) for p, py, px in plane]
    for cp in lo3:
        cp.wait_recv()
    row = add_all([l3[i] for i in range(NZ)])
    loss_o[...] = jnp.broadcast_to(jnp.sum(row, axis=1, keepdims=True) / BATCH, (1, 128))
    for cp in h3:
        cp.wait_recv()
    for i, j in order:
        gh_o[i * 48:(i + 1) * 48, j * 256:(j + 1) * 256] = g3r[i, j].astype(F32)
    for cp in stores:
        cp.wait()
    for cp in copies:
        cp.wait_send()


def place(loss_h, a, b, d, loss_o, a_o, b_o, d_o, loss_v, a_v, b_v, d_v, sems):
    ins = ((d, d_v), (a, a_v), (b, b_v), (loss_h, loss_v))
    loads = [pltpu.make_async_copy(p, q, sems.at[i]) for i, (p, q) in enumerate(ins)]
    outs = ((d_v, d_o), (a_v, a_o), (b_v, b_o))
    stores = [pltpu.make_async_copy(p, q, sems.at[4 + i]) for i, (p, q) in enumerate(outs)]
    for cp in loads:
        cp.start()
    for i in range(3):
        loads[i].wait()
        stores[i].start()
    loads[3].wait()
    loss_o[...] = loss_v[:, 0:1]
    for cp in stores:
        cp.wait()


def body(query_feat, key_feat, head_weight, pair):
    vmem = pl.BlockSpec(memory_space=pltpu.VMEM)
    hbm = pl.BlockSpec(memory_space=pl.ANY)
    V = pltpu.VMEM
    loss, gq, gk, gh = pl.pallas_call(
        kernel,
        out_shape=(
            jax.ShapeDtypeStruct((1, 128), F32),
            jax.ShapeDtypeStruct((FEAT, ROWS), BF16),
            jax.ShapeDtypeStruct((FEAT, ROWS), BF16),
            jax.ShapeDtypeStruct((FEAT, EMB), F32),
        ),
        in_specs=[hbm] * 4,
        out_specs=(vmem, hbm, hbm, vmem),
        scratch_shapes=[
            V((FEAT, ROWS), BF16), V((FEAT, ROWS), BF16),
            V((ROWS, FEAT), BF16), V((ROWS, FEAT), BF16), V((FEAT, EMB), BF16), V((2, 128), jnp.int32),
            V((FEAT, ROWS), BF16), V((FEAT, ROWS), BF16),
            V((4, 2, OWN, FEAT), BF16), V((4, FEAT, EMB), BF16),
            V((NZ, 1, 128), jnp.int32),
            V((NZ, OWN, EMB), BF16), V((NY, NX, 2, OWN, EMB), BF16),
            V((2, 8, 256, 256), F32), V((8, 256, 512), BF16),
            V((NZ, NZ, 1, 128), F32), V((NZ, 1, 128), F32),
            V((NZ, OWN, EMB), F32), V((2, 4, OWN, EMB), BF16), V((2, 4, OWN, EMB), BF16),
            V((NY, NX, 2, OWN, EMB), BF16), V((NY, NX, OWN, EMB), BF16), V((NY, NX, OWN, EMB), BF16),
            V((2, 4, 4, HALF, EMB), BF16), V((2, 4, HALF, EMB), BF16), V((2, 4, HALF, EMB), BF16),
            V((4, OWN, EMB), BF16), V((4, OWN, EMB), BF16),
            V((4, 2, 48, 256), BF16), V((4, 2, 48, 256), BF16),
            V((NZ, 48, 256), BF16), V((48, 256), BF16), V((4, 2, 48, 256), BF16),
            V((4, 1, 128), F32), V((4, 2, 1, 128), F32), V((NZ, 1, 128), F32),
            pltpu.SemaphoreType.DMA((N_SEMS,)), pltpu.SemaphoreType.DMA((N_SEMS,)), pltpu.SemaphoreType.DMA((4,)),
        ],
        compiler_params=pltpu.CompilerParams(collective_id=0, has_side_effects=True, vmem_limit_bytes=60 << 20),
    )(query_feat.T, key_feat.T, head_weight, pair.reshape(2, 128))
    loss, gq, gk, gh = pl.pallas_call(
        place,
        out_shape=(jax.ShapeDtypeStruct((1, 1), F32),) + tuple(
            jax.ShapeDtypeStruct(v.shape, v.dtype) for v in (gq, gk, gh)),
        in_specs=[hbm] * 4,
        out_specs=(vmem, hbm, hbm, hbm),
        scratch_shapes=[V(v.shape, v.dtype) for v in (loss, gq, gk, gh)] + [pltpu.SemaphoreType.DMA((8,))],
        compiler_params=pltpu.CompilerParams(vmem_limit_bytes=60 << 20),
    )(loss, gq, gk, gh)
    return loss.reshape(()), gq.T, gk.T, gh


def solution(mesh):
    shape = {"tp": (2, 2), "blk": (8, 4, 2)}
    names = {"tp": TP, "blk": BLK}
    a, b = mesh.axis_names
    fine = Mesh(mesh.devices.reshape(shape[a] + shape[b]), names[a] + names[b])
    in_specs = (P(BLK, TP), P(BLK, TP), P(TP, None), P(BLK))
    out_specs = (P(), P(BLK, TP), P(BLK, TP), P(TP, None))
    return jax.shard_map(body, mesh=fine, in_specs=in_specs, out_specs=out_specs, check_vma=False)
```

time: 92.3 us -> 82.8 us (0.90)
  local copies, waits for them, and re-layouts: 4.17 us -> 0 us
  Pallas kernels: 86.1 us -> 82.1 us
  between operations: 1.85 us -> 0.64 us
    pallas_call x1, Pallas kernels: 86.1 us -> 79.7 us  [body(): pl.pallas_call(kernel, out_shape=(jax.ShapeDtypeStruct((1, 128), F32), ja...]
    unnamed x9 -> x0, local copies, waits for them, and re-layouts: 3.37 us -> none
    pallas_call x0 -> x1, Pallas kernels: none -> 2.38 us  [body(): pl.pallas_call(place, out_shape=(jax.ShapeDtypeStruct((1, 1), F32),) + tu...]
where the time goes in v3:
time: 82.8 us; the launch traced here: 82.7 us
  Pallas kernels  82.1 us (99%)
    pallas_call x1, Pallas kernels, body(): pl.pallas_call(kernel, out_shape=(jax.ShapeDtypeStruct((1, 128), F32), ja...  79.7 us
    pallas_call x1, Pallas kernels, body(): pl.pallas_call(place, out_shape=(jax.ShapeDtypeStruct((1, 1), F32),) + tu...  2.38 us

profile of v3, /device:TPU:2, one launch (start us, length us, event | category | flops | bytes accessed | tf_op | source)
XLA Modules:
  0.0 82.7 jit_solution(16731504289730288107)
XLA Ops:
  0.6 79.7 %shard_map.75 = (f32[1,128]{1,0:T(1,128)}, bf16[192,256]{1,0:T(8,128)(2,1)}, bf16[192,256]{1,0:T(8,128)(2,1)}, f32[192,512]{1,0:T(8,128)}) custom-call(bf16[192,256]{1,0:T(8,128)(2,1)} %bitcast.6, bf16[192,256]{1,0:T(8,128)(2,1)} %bitcast.7, bf16[192,512]{1,0:T(8,128)(2,1)} %w_h.1, s32[2,128]{1,0:T(2,128)} %bitcast.8), custom_call_target="tpu_custom_call" | custom-call | tf_op jit(solution)/shard_map/pallas_call | solution.py:418
  80.3 2.4 %shard_map.76 = (f32[1,1]{1,0:T(1,128)}, bf16[192,256]{1,0:T(8,128)(2,1)}, bf16[192,256]{1,0:T(8,128)(2,1)}, f32[192,512]{1,0:T(8,128)}) custom-call(f32[1,128]{1,0:T(1,128)} %get-tuple-element.12.loss_h, bf16[192,256]{1,0:T(8,128)(2,1)} %get-tuple-element.13.a, bf16[192,256]{1,0:T(8,128)(2,1)} %get-tuple-element.14.b, f32[192,512]{1,0:T(8,128)} %get-tuple-element.15.d), custom_call_target="tpu_custom_call" | custom-call | tf_op jit(solution)/shard_map/pallas_call | solution.py:448

commit v4 on v3

v4 whole, which is shorter than its diff:
```python
import functools
import math

import jax
import jax.numpy as jnp
from jax import lax
from jax.experimental import pallas as pl
from jax.experimental.pallas import tpu as pltpu
from jax.sharding import Mesh, PartitionSpec as P

logit_gain = 3.0
TP = ("xlo", "core")
BLK = ("z", "y", "xh")
MESH = pl.DeviceIdType.MESH
F32 = jnp.float32
BF16 = jnp.bfloat16
NZ, NY, NX = 8, 4, 4
ROWS, OWN, EMB, FEAT = 256, 64, 512, 192
HALF = OWN // 2
BATCH = 16384
SCALE = logit_gain / math.sqrt(EMB)
N_SEMS = 192
NT = (((1,), (1,)), ((), ()))
TN = (((0,), (0,)), ((), ()))


OFF = (0, 1, 7, 2, 6, 3, 5, 4)
SLOT = {o: k for k, o in enumerate(OFF)}
FAR = (4, 3, 5, 2, 6, 1, 7)


def add_all(values):
    return functools.reduce(jnp.add, values)


def kernel(xq_h, xk_h, w_h, pair_h, loss_o, gq_h, gk_h, gh_o,
           xqt, xkt, xq, xk, w, pair, f, wb, pbuf, zqa, zka, st, wt, lbuf, lsum,
           dqf, zs, zr, dk, ck, pk, k1, k2s, k2, dq4, dk4,
           gs, g1r, g2r, g3s, g3r, l1, l2, l3, ss, rs, ls):
    z, y, xh, xlo, c = [lax.axis_index(a) for a in ("z", "y", "xh", "xlo", "core")]
    x = 2 * xh + xlo
    t = 2 * xlo + c
    oc, oxlo, oxh = 1 - c, 1 - xlo, 1 - xh

    loads = [pltpu.make_async_copy(a, b, ls.at[i]) for i, (a, b) in enumerate(
        ((xq_h, xqt), (xk_h, xkt), (w_h, w), (pair_h, pair)))]
    for cp in loads:
        cp.start()

    def at_z(d):
        return lax.rem(z + d, NZ)

    def at_y(d):
        return lax.rem(y + d, NY)

    def at_x(d):
        return lax.rem(x + d, NX)

    def dev_x(d):
        v = at_x(d)
        return {"xh": v // 2, "xlo": lax.rem(v, 2)}

    core_dev = {"core": oc}
    partner = {"xlo": oxlo}
    other = {"xlo": oxlo, "xh": oxh}
    cross = {"xlo": oxlo, "core": oc}
    z_dev = [{"z": at_z(d)} for d in range(NZ)]
    y_dev = [{"y": at_y(d)} for d in range(NY)]
    x_dev = [dev_x(d) for d in range(NX)]
    diag = [{"y": at_y(d), "xh": oxh} for d in range(NY)]

    peers = [z_dev[1], z_dev[7]] + y_dev[1:] + x_dev[1:] + [core_dev, cross]
    barrier = pltpu.get_barrier_semaphore()
    for p in peers:
        pl.semaphore_signal(barrier, inc=1, device_id=p, device_id_type=MESH)
    for cp in loads:
        cp.wait()
    xq[...] = xqt[...].T
    xk[...] = xkt[...].T
    pl.semaphore_wait(barrier, len(peers))

    copies = []
    settled = [0]

    def settle(upto):
        for cp in copies[settled[0]:upto]:
            cp.wait_send()
        settled[0] = upto

    def send(src, dst, dev):
        i = len(copies)
        cp = pltpu.make_async_remote_copy(src_ref=src, dst_ref=dst, send_sem=ss.at[i], recv_sem=rs.at[i],
                                          device_id=dev, device_id_type=MESH)
        cp.start()
        copies.append(cp)
        return cp

    def rows_of(a, b):
        return pl.ds((2 * a + b) * OWN, OWN)

    feats = ((xq, 0), (xk, 1))
    W = [pl.ds(48 * i, 48) for i in range(4)]
    f2 = [send(r.at[rows_of(oxlo, c)], f.at[2, i], partner) for r, i in feats]
    w2 = {i: send(w.at[W[i]], wb.at[2, W[i]], other) for i in (1, 2, 3)}
    f3 = [send(r.at[rows_of(oxlo, oc)], f.at[3, i], cross) for r, i in feats]
    w2[0] = send(w.at[W[0]], wb.at[2, W[0]], partner)
    f1 = [send(r.at[rows_of(xlo, oc)], f.at[1, i], core_dev) for r, i in feats]
    w1 = send(w, wb.at[1], core_dev)

    own = rows_of(xlo, c)

    def project(rows, weights):
        return jnp.dot(rows, weights, preferred_element_type=F32)

    acc = project(jnp.concatenate([xq[own, :], xk[own, :]], axis=0), w[...])
    for cp in f1:
        cp.wait_recv()
    w1.wait_recv()
    acc += project(f[1].reshape(2 * OWN, FEAT), wb[1])
    w3 = []
    for i in (1, 2, 0, 3):
        w2[i].wait_recv()
        w3.append(send(wb.at[2, W[i]], wb.at[3, W[i]], core_dev))
    for cp in f2:
        cp.wait_recv()
    acc += project(f[2].reshape(2 * OWN, FEAT), wb[2])
    for cp in f3 + w3:
        cp.wait_recv()
    acc += project(f[3].reshape(2 * OWN, FEAT), wb[3])
    zqa[0] = acc[:OWN].astype(BF16)
    zka[0, y, c, x] = acc[OWN:OWN + HALF].astype(BF16)
    zka[1, x, c, y] = acc[OWN + HALF:].astype(BF16)

    H = (pl.ds(0, HALF), pl.ds(HALF, HALF))
    ALL = pl.ds(0, OWN)
    up, down = z_dev[1], z_dev[NZ - 1]
    home = (y, x)
    mine = (zka.at[0, y, c, x], zka.at[1, x, c, y])

    def ring_send(s, part=ALL):
        a, b = SLOT[(NZ - s + 1) % NZ], SLOT[s - 1]
        a2, b2 = SLOT[NZ - s], SLOT[s]
        pa, pb = (H[0], H[1]) if s == 4 else (ALL, ALL)
        return (send(zqa.at[a, pa], zqa.at[a2, pa], up), send(zqa.at[b, pb], zqa.at[b2, pb], down))

    NEAR = (2, 1, 3)
    r1 = ring_send(1)
    first = (x_dev, y_dev)
    second = (y_dev, x_dev)
    turn = (at_y, at_x)
    k1st = [{d: send(mine[h], mine[h], first[h][d]) for d in NEAR} for h in range(2)]
    k2nd = [{d: [] for d in NEAR} for h in range(2)]

    def spread(h, r):
        for d in NEAR:
            k2nd[h][d].append(send(r, r, second[h][d]))

    kc = {}

    def to_core(d):
        for h in range(2):
            for cp in k2nd[h][d] if d else ():
                cp.wait_recv()
            r = zka.at[h, turn[h](4 - d), c]
            kc[d, h] = send(r, r, core_dev)

    stats = ([], [])

    def score(d, g):
        q = zqa[pl.ds(4 * g, 4)].reshape(256, EMB)
        for h in range(2):
            a = turn[h](4 - d)
            v = SCALE * lax.dot_general(zka[h, a].reshape(256, EMB), q, NT, preferred_element_type=F32)
            m = jnp.max(v, axis=0, keepdims=True)
            st[g, h * 4 + a] = v
            stats[g].append((m, jnp.sum(jnp.exp(v - m), axis=0, keepdims=True)))

    def from_core(d):
        for h in range(2):
            kc[d, h].wait_recv()

    def merged(g):
        m = functools.reduce(jnp.maximum, [p[0] for p in stats[g]])
        return m + jnp.log(add_all([p[1] * jnp.exp(p[0] - m) for p in stats[g]]))

    lane = lax.broadcasted_iota(jnp.int32, (1, 128), 1)
    low = lane < OWN

    def put_parts(g, row):
        for j in range(2):
            v = row[:, 128 * j:128 * j + 128]
            turned = pltpu.roll(v, OWN, 1)
            lbuf[z, at_z(OFF[4 * g + 2 * j])] = jnp.where(low, v, turned)
            lbuf[z, at_z(OFF[4 * g + 2 * j + 1])] = jnp.where(low, turned, v)

    for h in range(2):
        spread(h, mine[h])
    for cp in r1:
        cp.wait_recv()
    r2 = ring_send(2)
    for d in (1, 3, 2):
        for h in range(2):
            k1st[h][d].wait_recv()
            b = turn[1 - h](4 - d)
            spread(h, zka.at[h, home[h], c, b])
    to_core(0)
    for cp in r2:
        cp.wait_recv()
    r3 = ring_send(3)
    from_core(0)
    score(0, 0)
    to_core(1)
    for cp in r3:
        cp.wait_recv()
    r4 = ring_send(4)
    to_core(3)
    from_core(1)
    score(1, 0)
    to_core(2)
    from_core(3)
    score(3, 0)
    for cp in r4:
        cp.wait_recv()
    for d in (0, 1, 3):
        score(d, 1)
    from_core(2)
    score(2, 0)
    score(2, 1)
    put_parts(0, merged(0))
    put_parts(1, merged(1))
    sent = len(copies)
    lc = [send(lbuf.at[z], lbuf.at[z], z_dev[d]) for d in FAR]
    prow = pair[pl.ds(xlo, 1), :]
    pbuf[z] = jnp.where((lane // OWN) == c, prow, pltpu.roll(prow, OWN, 1))
    pc = [send(pbuf.at[z], pbuf.at[z], z_dev[d]) for d in FAR]
    settle(sent)
    for cp in lc + pc:
        cp.wait_recv()
    for i in range(NZ):
        parts = [lbuf[k, i] for k in range(NZ)]
        m = functools.reduce(jnp.maximum, parts)
        lsum[i] = m + jnp.log(add_all([jnp.exp(p - m) for p in parts]))

    def in_order(at):
        return [jnp.concatenate([jnp.where(low, at(at_z(OFF[4 * g + 2 * j])), at(at_z(OFF[4 * g + 2 * j + 1])))
                                 for j in range(2)], axis=1) for g in range(2)]

    lse = in_order(lambda i: lsum[i])
    pairs = [p - z * 2048 for p in in_order(lambda i: pbuf[i])]

    FAC = SCALE / BATCH
    zq = zqa[...].reshape(NZ * OWN, EMB)
    row = lax.broadcasted_iota(jnp.int32, (256, 256), 0)
    core_row = (row // 128) * 64 + row % 32
    peer_row = (row // 32) % 4
    pos = (jnp.zeros((1, 256), F32),) * 2
    for h in range(2):
        ids = core_row + peer_row * (128, 512)[h] + 32 * h

        def weight_step(a, pos, h=h, ids=ids):
            new = []
            for g in range(2):
                v = st[g, h * 4 + a]
                hit = ids == pairs[g] - a * (512, 128)[h]
                e = jnp.exp(v - lse[g])
                wt[h * 4 + a, :, 256 * g:256 * g + 256] = jnp.where(hit, e - 1.0, e).astype(BF16)
                new.append(pos[g] + jnp.sum(jnp.where(hit, v, 0.0), axis=0, keepdims=True))
            return tuple(new)

        pos = lax.fori_loop(0, 4, weight_step, pos)

    def query_rows(g):
        wg = wt[:, :, 256 * g:256 * g + 256].reshape(2048, 256)
        v = lax.dot_general(wg, zka[...].reshape(2048, EMB), TN, preferred_element_type=F32) * FAC
        dqf[pl.ds(4 * g, 4)] = v.reshape(4, OWN, EMB)

    query_rows(1)
    def ahead(dr, d):
        return d if dr == 0 else NZ - d

    zc = {}
    for dr in range(2):
        zs[dr, 1, H[dr], :] = dqf[SLOT[4], H[dr], :].astype(BF16)
        zc[dr, 1] = send(zs.at[dr, 1, H[dr]], zr.at[dr, 1, H[dr]], z_dev[ahead(dr, 2)])
        zs[dr, 0] = dqf[SLOT[ahead(dr, 3)]].astype(BF16)
        zc[dr, 0] = send(zs.at[dr, 0], zr.at[dr, 0], z_dev[ahead(dr, 1)])

    kcs = {}

    def key_rows(d, h):
        a = turn[h](d)
        v = jnp.dot(wt[h * 4 + a], zq, preferred_element_type=F32) * FAC
        dk[h, a] = v.astype(BF16).reshape(2, 4, HALF, EMB)
        kcs[d, h] = send(dk.at[h, a, oc], ck.at[h, a], core_dev)

    k1c = ([], [])

    def core_sum(d, h):
        a = turn[h](d)
        kcs[d, h].wait_recv()
        v = (dk[h, a, c].astype(F32) + ck[h, a].astype(F32)).astype(BF16)
        if d:
            pk[h, a] = v
            k1c[h].append(send(pk.at[h, a], k1.at[h, home[h]], second[h][d]))
        else:
            k1[h, a] = v

    steps = [(d, h) for d in (2, 1, 3, 0) for h in range(2)]
    for n, (d, h) in enumerate(steps):
        key_rows(d, h)
        if n >= 3:
            core_sum(*steps[n - 3])
    for n in (5, 6, 7):
        core_sum(*steps[n])
    query_rows(0)
    for dr in range(2):
        zs[dr, 2] = dqf[SLOT[ahead(dr, 1)]].astype(BF16)
        zc[dr, 2] = send(zs.at[dr, 2], zr.at[dr, 2], z_dev[ahead(dr, 1)])
    lanes0 = jnp.where(low, lse[0][:, :128], 0.0)
    l1[t] = lanes0 - add_all([p[:, 128 * j:128 * j + 128] for p in pos for j in range(2)])
    lo1 = [send(l1.at[t], l1.at[t], p) for p in (core_dev, partner, cross)]
    for dr in range(2):
        v = dqf[SLOT[ahead(dr, 2)]]
        zc[dr, 0].wait_recv()
        v += zr[dr, 0].astype(F32)
        zc[dr, 1].wait_recv()
        pieces = [v[:HALF], v[HALF:]]
        pieces[dr] += zr[dr, 1, H[dr], :].astype(F32)
        for h in range(2):
            zs[dr, 3, H[h], :] = pieces[h].astype(BF16)
        zc[dr, 3] = send(zs.at[dr, 3], zr.at[dr, 3], z_dev[ahead(dr, 2)])
    k2c = []
    for h in range(2):
        for cp in k1c[h]:
            cp.wait_recv()
        k2s[h] = add_all([k1[h, i].astype(F32) for i in range(4)]).astype(BF16)
        me = home[1 - h]
        k2c += [send(k2s.at[h, turn[1 - h](d)], k2.at[h, me], first[h][d]) for d in NEAR]
        k2[h, me] = k2s[h, me]
    v = dqf[0]
    for dr in range(2):
        for i in (2, 3):
            zc[dr, i].wait_recv()
            v += zr[dr, i].astype(F32)
    dq4[t] = v.astype(BF16)
    tpt = 2 * oxlo + c
    q1 = send(dq4.at[t], dq4.at[t], partner)
    q2 = send(dq4.at[t], dq4.at[t], core_dev)
    d1, d2 = [], []
    for h in range(2):
        for cp in k2c[3 * h:3 * h + 3]:
            cp.wait_recv()
        dk4[t, H[h], :] = add_all([k2[h, i].astype(F32) for i in range(4)]).astype(BF16)
        r = dk4.at[t, H[h]]
        d1.append(send(r, r, partner))
        d2.append(send(r, r, core_dev))
    q1.wait_recv()
    q3 = send(dq4.at[tpt], dq4.at[tpt], core_dev)
    d3 = []
    for h in range(2):
        d1[h].wait_recv()
        r = dk4.at[tpt, H[h]]
        d3.append(send(r, r, core_dev))
    for cp in (q2, q3):
        cp.wait_recv()
    dq = dq4[...].reshape(ROWS, EMB)
    head = jnp.dot(xqt[...], dq, preferred_element_type=F32)
    for cp in d2 + d3:
        cp.wait_recv()
    dkv = dk4[...].reshape(ROWS, EMB)
    head += jnp.dot(xkt[...], dkv, preferred_element_type=F32)

    for i in range(4):
        for j in range(2):
            gs[i, j] = head[i * 48:(i + 1) * 48, j * 256:(j + 1) * 256].astype(BF16)
    plane = [(diag[2], at_y(2), oxh), (diag[1], at_y(1), oxh), (diag[3], at_y(3), oxh), (y_dev[2], at_y(2), xh),
             ({"xh": oxh}, y, oxh), (y_dev[1], at_y(1), xh), (y_dev[3], at_y(3), xh)]
    sent = len(copies)
    h1 = [send(gs.at[py, px], g1r.at[y, xh], p) for p, py, px in plane]
    for cp in lo1:
        cp.wait_recv()
    l2[y, xh] = l1[0] + l1[1] + l1[2] + l1[3]
    lo2 = [send(l2.at[y, xh], l2.at[y, xh], p) for p, py, px in plane]
    gq_h[...] = lax.dot_general(w[...], dq, NT, preferred_element_type=F32).astype(BF16)
    gk_h[...] = lax.dot_general(w[...], dkv, NT, preferred_element_type=F32).astype(BF16)
    g1r[y, xh] = gs[y, xh]
    settle(sent)
    for cp in h1:
        cp.wait_recv()
    order = [(i, j) for i in range(4) for j in range(2)]
    g2r[z] = add_all([g1r[i, j].astype(F32) for i, j in order]).astype(BF16)
    sent = len(copies)
    h2 = [send(g2r.at[z], g2r.at[z], z_dev[d]) for d in FAR]
    for cp in lo2:
        cp.wait_recv()
    l3[z] = add_all([l2[i, j] for i, j in order])
    lo3 = [send(l3.at[z], l3.at[z], z_dev[d]) for d in FAR]
    settle(sent)
    for cp in h2:
        cp.wait_recv()
    g3s[...] = add_all([g2r[i].astype(F32) for i in range(NZ)]).astype(BF16)
    g3r[y, xh] = g3s[...]
    sent = len(copies)
    h3 = [send(g3s, g3r.at[y, xh], p) for p, py, px in plane]
    for cp in lo3:
        cp.wait_recv()
    row = add_all([l3[i] for i in range(NZ)])
    loss_o[...] = jnp.broadcast_to(jnp.sum(row, axis=1, keepdims=True) / BATCH, (1, 128))
    settle(sent)
    for cp in h3:
        cp.wait_recv()
    for i, j in order:
        gh_o[i * 48:(i + 1) * 48, j * 256:(j + 1) * 256] = g3r[i, j].astype(F32)
    settle(len(copies))


def body(query_feat, key_feat, head_weight, pair):
    vmem = pl.BlockSpec(memory_space=pltpu.VMEM)
    hbm = pl.BlockSpec(memory_space=pl.ANY)
    V = pltpu.VMEM
    loss, gq, gk, gh = pl.pallas_call(
        kernel,
        out_shape=(
            jax.ShapeDtypeStruct((1, 128), F32),
            V((FEAT, ROWS), BF16),
            V((FEAT, ROWS), BF16),
            V((FEAT, EMB), F32),
        ),
        in_specs=[hbm] * 4,
        out_specs=(vmem, vmem, vmem, vmem),
        scratch_shapes=[
            V((FEAT, ROWS), BF16), V((FEAT, ROWS), BF16),
            V((ROWS, FEAT), BF16), V((ROWS, FEAT), BF16), V((FEAT, EMB), BF16), V((2, 128), jnp.int32),
            V((4, 2, OWN, FEAT), BF16), V((4, FEAT, EMB), BF16),
            V((NZ, 1, 128), jnp.int32),
            V((NZ, OWN, EMB), BF16), V((2, 4, 2, 4, HALF, EMB), BF16),
            V((2, 8, 256, 256), F32), V((8, 256, 512), BF16),
            V((NZ, NZ, 1, 128), F32), V((NZ, 1, 128), F32),
            V((NZ, OWN, EMB), F32), V((2, 4, OWN, EMB), BF16), V((2, 4, OWN, EMB), BF16),
            V((2, 4, 2, 4, HALF, EMB), BF16), V((2, 4, 4, HALF, EMB), BF16), V((2, 4, 4, HALF, EMB), BF16),
            V((2, 4, 4, HALF, EMB), BF16), V((2, 4, HALF, EMB), BF16), V((2, 4, HALF, EMB), BF16),
            V((4, OWN, EMB), BF16), V((4, OWN, EMB), BF16),
            V((4, 2, 48, 256), BF16), V((4, 2, 48, 256), BF16),
            V((NZ, 48, 256), BF16), V((48, 256), BF16), V((4, 2, 48, 256), BF16),
            V((4, 1, 128), F32), V((4, 2, 1, 128), F32), V((NZ, 1, 128), F32),
            pltpu.SemaphoreType.DMA((N_SEMS,)), pltpu.SemaphoreType.DMA((N_SEMS,)), pltpu.SemaphoreType.DMA((4,)),
        ],
        compiler_params=pltpu.CompilerParams(collective_id=0, has_side_effects=True, vmem_limit_bytes=44 << 20),
    )(*[pltpu.with_memory_space_constraint(v, pltpu.HBM) for v in (
        query_feat.T, key_feat.T, head_weight, pair.reshape(2, 128))])
    return loss[0, 0], gq.T, gk.T, gh


def solution(mesh):
    shape = {"tp": (2, 2), "blk": (8, 4, 2)}
    names = {"tp": TP, "blk": BLK}
    a, b = mesh.axis_names
    fine = Mesh(mesh.devices.reshape(shape[a] + shape[b]), names[a] + names[b])
    in_specs = (P(BLK, TP), P(BLK, TP), P(TP, None), P(BLK))
    out_specs = (P(), P(BLK, TP), P(BLK, TP), P(TP, None))
    return jax.shard_map(body, mesh=fine, in_specs=in_specs, out_specs=out_specs, check_vma=False)
```

time: 82.8 us -> 81.8 us (0.988)
  Pallas kernels: 82.1 us -> 77.7 us
  local copies, waits for them, and re-layouts: 0 us -> 2.03 us
  between operations: 0.64 us -> 1.81 us
    pallas_call x2 -> x1, Pallas kernels: 82.1 us -> 77.7 us  [body(): pl.pallas_call(kernel, out_shape=(jax.ShapeDtypeStruct((1, 128), F32), V(...]
    unnamed x0 -> x3, local copies, waits for them, and re-layouts: none -> 2.03 us
where the time goes in v4:
time: 81.8 us; the launch traced here: 81.5 us
  Pallas kernels  77.7 us (95%)
  local copies, waits for them, and re-layouts  2.03 us (2%)
  between operations  1.81 us (2%)
    pallas_call x1, Pallas kernels, body(): pl.pallas_call(kernel, out_shape=(jax.ShapeDtypeStruct((1, 128), F32), V(...  77.7 us
    unnamed x3, local copies, waits for them, and re-layouts  2.03 us

profile of v4, /device:TPU:2, one launch (start us, length us, event | category | flops | bytes accessed | tf_op | source)
XLA Modules:
  0.0 81.5 jit_solution(18081457783463665524)
XLA Ops:
  0.6 77.7 %shard_map.75 = (f32[1,128]{1,0:T(1,128)S(1)}, bf16[192,256]{1,0:T(8,128)(2,1)S(1)}, bf16[192,256]{1,0:T(8,128)(2,1)S(1)}, f32[192,512]{1,0:T(8,128)S(1)}) custom-call(bf16[192,256]{1,0:T(8,128)(2,1)} %bitcast.10, bf16[192,256]{1,0:T(8,128)(2,1)} %bitcast.11, bf16[192,512]{1,0:T(8,128)(2,1)} %w_h.1, s32[2,128]{1,0:T(2,128)} %bitcast.12), custom_call_target="tpu_custom_call" | custom-call | tf_op jit(solution)/shard_map/pallas_call | solution.py:421
  78.3 0.6 copy.12
  78.9 0.6 copy.13
  79.6 0.7 copy.14

commit v5 on v4

--- a/solution.py
+++ b/solution.py
@@ -69,7 +69,7 @@
     x_dev = [dev_x(d) for d in range(NX)]
     diag = [{"y": at_y(d), "xh": oxh} for d in range(NY)]
 
-    peers = [z_dev[1], z_dev[7]] + y_dev[1:] + x_dev[1:] + [core_dev, cross]
+    peers = [z_dev[1], z_dev[2], z_dev[6], z_dev[7]] + y_dev[1:] + x_dev[1:] + [core_dev, cross]
     barrier = pltpu.get_barrier_semaphore()
     for p in peers:
         pl.semaphore_signal(barrier, inc=1, device_id=p, device_id_type=MESH)
@@ -133,18 +133,15 @@
 
     H = (pl.ds(0, HALF), pl.ds(HALF, HALF))
     ALL = pl.ds(0, OWN)
-    up, down = z_dev[1], z_dev[NZ - 1]
     home = (y, x)
     mine = (zka.at[0, y, c, x], zka.at[1, x, c, y])
 
-    def ring_send(s, part=ALL):
-        a, b = SLOT[(NZ - s + 1) % NZ], SLOT[s - 1]
-        a2, b2 = SLOT[NZ - s], SLOT[s]
-        pa, pb = (H[0], H[1]) if s == 4 else (ALL, ALL)
-        return (send(zqa.at[a, pa], zqa.at[a2, pa], up), send(zqa.at[b, pb], zqa.at[b2, pb], down))
+    def pass_on(k, part, d):
+        return send(zqa.at[SLOT[k % NZ], part], zqa.at[SLOT[(k - d) % NZ], part], z_dev[d % NZ])
 
     NEAR = (2, 1, 3)
-    r1 = ring_send(1)
+    r2 = [pass_on(0, ALL, d) for d in (2, -2)]
+    r1 = [pass_on(0, ALL, d) for d in (1, -1)]
     first = (x_dev, y_dev)
     second = (y_dev, x_dev)
     turn = (at_y, at_x)
@@ -190,29 +187,27 @@
         for j in range(2):
             v = row[:, 128 * j:128 * j + 128]
             turned = pltpu.roll(v, OWN, 1)
-            lbuf[z, at_z(OFF[4 * g + 2 * j])] = jnp.where(low, v, turned)
-            lbuf[z, at_z(OFF[4 * g + 2 * j + 1])] = jnp.where(low, turned, v)
+            lbuf[z, pl.ds(at_z(OFF[4 * g + 2 * j]), 1), :] = jnp.where(low, v, turned)
+            lbuf[z, pl.ds(at_z(OFF[4 * g + 2 * j + 1]), 1), :] = jnp.where(low, turned, v)
 
     for h in range(2):
         spread(h, mine[h])
-    for cp in r1:
-        cp.wait_recv()
-    r2 = ring_send(2)
     for d in (1, 3, 2):
         for h in range(2):
             k1st[h][d].wait_recv()
             b = turn[1 - h](4 - d)
             spread(h, zka.at[h, home[h], c, b])
     to_core(0)
-    for cp in r2:
-        cp.wait_recv()
-    r3 = ring_send(3)
+    r4 = []
+    for i, d in enumerate((1, -1)):
+        r2[i].wait_recv()
+        r4.append(pass_on(-2 * d, H[i], 2 * d))
+        r4.append(pass_on(-2 * d, ALL, d))
+    for cp in r1:
+        cp.wait_recv()
     from_core(0)
     score(0, 0)
     to_core(1)
-    for cp in r3:
-        cp.wait_recv()
-    r4 = ring_send(4)
     to_core(3)
     from_core(1)
     score(1, 0)
@@ -221,6 +216,9 @@
     score(3, 0)
     for cp in r4:
         cp.wait_recv()
+    prow = pair[pl.ds(xlo, 1), :]
+    pbuf[z] = jnp.where((lane // OWN) == c, prow, pltpu.roll(prow, OWN, 1))
+    pc = [send(pbuf.at[z], pbuf.at[z], z_dev[d]) for d in FAR]
     for d in (0, 1, 3):
         score(d, 1)
     from_core(2)
@@ -230,22 +228,18 @@
     put_parts(1, merged(1))
     sent = len(copies)
     lc = [send(lbuf.at[z], lbuf.at[z], z_dev[d]) for d in FAR]
-    prow = pair[pl.ds(xlo, 1), :]
-    pbuf[z] = jnp.where((lane // OWN) == c, prow, pltpu.roll(prow, OWN, 1))
-    pc = [send(pbuf.at[z], pbuf.at[z], z_dev[d]) for d in FAR]
     settle(sent)
     for cp in lc + pc:
         cp.wait_recv()
-    for i in range(NZ):
-        parts = [lbuf[k, i] for k in range(NZ)]
-        m = functools.reduce(jnp.maximum, parts)
-        lsum[i] = m + jnp.log(add_all([jnp.exp(p - m) for p in parts]))
+    parts = [lbuf[k] for k in range(NZ)]
+    m = functools.reduce(jnp.maximum, parts)
+    lsum[...] = m + jnp.log(add_all([jnp.exp(p - m) for p in parts]))
 
     def in_order(at):
         return [jnp.concatenate([jnp.where(low, at(at_z(OFF[4 * g + 2 * j])), at(at_z(OFF[4 * g + 2 * j + 1])))
                                  for j in range(2)], axis=1) for g in range(2)]
 
-    lse = in_order(lambda i: lsum[i])
+    lse = in_order(lambda i: lsum[pl.ds(i, 1), :])
     pairs = [p - z * 2048 for p in in_order(lambda i: pbuf[i])]
 
     FAC = SCALE / BATCH
@@ -253,22 +247,24 @@
     row = lax.broadcasted_iota(jnp.int32, (256, 256), 0)
     core_row = (row // 128) * 64 + row % 32
     peer_row = (row // 32) % 4
-    pos = (jnp.zeros((1, 256), F32),) * 2
-    for h in range(2):
-        ids = core_row + peer_row * (128, 512)[h] + 32 * h
-
-        def weight_step(a, pos, h=h, ids=ids):
-            new = []
-            for g in range(2):
+    pos = []
+
+    def weights_of(g):
+        total = jnp.zeros((1, 256), F32)
+        for h in range(2):
+            ids = core_row + peer_row * (128, 512)[h] + 32 * h
+
+            def weight_step(a, total, h=h, ids=ids):
                 v = st[g, h * 4 + a]
                 hit = ids == pairs[g] - a * (512, 128)[h]
                 e = jnp.exp(v - lse[g])
                 wt[h * 4 + a, :, 256 * g:256 * g + 256] = jnp.where(hit, e - 1.0, e).astype(BF16)
-                new.append(pos[g] + jnp.sum(jnp.where(hit, v, 0.0), axis=0, keepdims=True))
-            return tuple(new)
-
-        pos = lax.fori_loop(0, 4, weight_step, pos)
-
+                return total + jnp.sum(jnp.where(hit, v, 0.0), axis=0, keepdims=True)
+
+            total = lax.fori_loop(0, 4, weight_step, total)
+        pos.append(total)
+
+    weights_of(1)
     def query_rows(g):
         wg = wt[:, :, 256 * g:256 * g + 256].reshape(2048, 256)
         v = lax.dot_general(wg, zka[...].reshape(2048, EMB), TN, preferred_element_type=F32) * FAC
@@ -282,8 +278,12 @@
     for dr in range(2):
         zs[dr, 1, H[dr], :] = dqf[SLOT[4], H[dr], :].astype(BF16)
         zc[dr, 1] = send(zs.at[dr, 1, H[dr]], zr.at[dr, 1, H[dr]], z_dev[ahead(dr, 2)])
-        zs[dr, 0] = dqf[SLOT[ahead(dr, 3)]].astype(BF16)
-        zc[dr, 0] = send(zs.at[dr, 0], zr.at[dr, 0], z_dev[ahead(dr, 1)])
+    for n in range(2):
+        for dr in range(2):
+            h = H[1 - dr if n == 0 else dr]
+            zs[dr, 0, h, :] = dqf[SLOT[ahead(dr, 3)], h, :].astype(BF16)
+            zc[dr, 0, n] = send(zs.at[dr, 0, h], zr.at[dr, 0, h], z_dev[ahead(dr, 1)])
+    weights_of(0)
 
     kcs = {}
 
@@ -319,16 +319,16 @@
     lanes0 = jnp.where(low, lse[0][:, :128], 0.0)
     l1[t] = lanes0 - add_all([p[:, 128 * j:128 * j + 128] for p in pos for j in range(2)])
     lo1 = [send(l1.at[t], l1.at[t], p) for p in (core_dev, partner, cross)]
-    for dr in range(2):
-        v = dqf[SLOT[ahead(dr, 2)]]
-        zc[dr, 0].wait_recv()
-        v += zr[dr, 0].astype(F32)
-        zc[dr, 1].wait_recv()
-        pieces = [v[:HALF], v[HALF:]]
-        pieces[dr] += zr[dr, 1, H[dr], :].astype(F32)
-        for h in range(2):
-            zs[dr, 3, H[h], :] = pieces[h].astype(BF16)
-        zc[dr, 3] = send(zs.at[dr, 3], zr.at[dr, 3], z_dev[ahead(dr, 2)])
+    for n in range(2):
+        for dr in range(2):
+            h = H[1 - dr if n == 0 else dr]
+            zc[dr, 0, n].wait_recv()
+            v = dqf[SLOT[ahead(dr, 2)], h, :] + zr[dr, 0, h, :].astype(F32)
+            if n == 1:
+                zc[dr, 1].wait_recv()
+                v += zr[dr, 1, h, :].astype(F32)
+            zs[dr, 3, h, :] = v.astype(BF16)
+            zc[dr, 3, n] = send(zs.at[dr, 3, h], zr.at[dr, 3, h], z_dev[ahead(dr, 2)])
     k2c = []
     for h in range(2):
         for cp in k1c[h]:
@@ -337,15 +337,19 @@
         me = home[1 - h]
         k2c += [send(k2s.at[h, turn[1 - h](d)], k2.at[h, me], first[h][d]) for d in NEAR]
         k2[h, me] = k2s[h, me]
-    v = dqf[0]
+    tpt = 2 * oxlo + c
     for dr in range(2):
-        for i in (2, 3):
-            zc[dr, i].wait_recv()
-            v += zr[dr, i].astype(F32)
-    dq4[t] = v.astype(BF16)
-    tpt = 2 * oxlo + c
-    q1 = send(dq4.at[t], dq4.at[t], partner)
-    q2 = send(dq4.at[t], dq4.at[t], core_dev)
+        zc[dr, 2].wait_recv()
+    for n in range(2):
+        for dr in range(2):
+            zc[dr, 3, n].wait_recv()
+    q1, q2 = [], []
+    for h in range(2):
+        dq4[t, H[h], :] = (dqf[0, H[h], :] + add_all(
+            [zr[dr, i, H[h], :].astype(F32) for dr in range(2) for i in (2, 3)])).astype(BF16)
+        r = dq4.at[t, H[h]]
+        q1.append(send(r, r, partner))
+        q2.append(send(r, r, core_dev))
     d1, d2 = [], []
     for h in range(2):
         for cp in k2c[3 * h:3 * h + 3]:
@@ -354,14 +358,17 @@
         r = dk4.at[t, H[h]]
         d1.append(send(r, r, partner))
         d2.append(send(r, r, core_dev))
-    q1.wait_recv()
-    q3 = send(dq4.at[tpt], dq4.at[tpt], core_dev)
+    q3 = []
+    for h in range(2):
+        q1[h].wait_recv()
+        r = dq4.at[tpt, H[h]]
+        q3.append(send(r, r, core_dev))
     d3 = []
     for h in range(2):
         d1[h].wait_recv()
         r = dk4.at[tpt, H[h]]
         d3.append(send(r, r, core_dev))
-    for cp in (q2, q3):
+    for cp in q2 + q3:
         cp.wait_recv()
     dq = dq4[...].reshape(ROWS, EMB)
     head = jnp.dot(xqt[...], dq, preferred_element_type=F32)
@@ -435,7 +442,7 @@
             V((NZ, 1, 128), jnp.int32),
             V((NZ, OWN, EMB), BF16), V((2, 4, 2, 4, HALF, EMB), BF16),
             V((2, 8, 256, 256), F32), V((8, 256, 512), BF16),
-            V((NZ, NZ, 1, 128), F32), V((NZ, 1, 128), F32),
+            V((NZ, NZ, 128), F32), V((NZ, 128), F32),
             V((NZ, OWN, EMB), F32), V((2, 4, OWN, EMB), BF16), V((2, 4, OWN, EMB), BF16),
             V((2, 4, 2, 4, HALF, EMB), BF16), V((2, 4, 4, HALF, EMB), BF16), V((2, 4, 4, HALF, EMB), BF16),
             V((2, 4, 4, HALF, EMB), BF16), V((2, 4, HALF, EMB), BF16), V((2, 4, HALF, EMB), BF16),

time: 81.8 us -> 79.1 us (0.967)
  Pallas kernels: 77.7 us -> 74.5 us
    pallas_call x1, Pallas kernels: 77.7 us -> 74.5 us  [body(): pl.pallas_call(kernel, out_shape=(jax.ShapeDtypeStruct((1, 128), F32), V(...]
where the time goes in v5:
time: 79.1 us; the launch traced here: 78.3 us
  Pallas kernels  74.5 us (94%)
  local copies, waits for them, and re-layouts  2.03 us (3%)
  between operations  1.81 us (2%)
    pallas_call x1, Pallas kernels, body(): pl.pallas_call(kernel, out_shape=(jax.ShapeDtypeStruct((1, 128), F32), V(...  74.5 us
    unnamed x3, local copies, waits for them, and re-layouts  2.03 us

profile of v5, /device:TPU:2, one launch (start us, length us, event | category | flops | bytes accessed | tf_op | source)
XLA Modules:
  0.0 78.3 jit_solution(13863881440742260700)
XLA Ops:
  0.6 74.5 %shard_map.75 = (f32[1,128]{1,0:T(1,128)S(1)}, bf16[192,256]{1,0:T(8,128)(2,1)S(1)}, bf16[192,256]{1,0:T(8,128)(2,1)S(1)}, f32[192,512]{1,0:T(8,128)S(1)}) custom-call(bf16[192,256]{1,0:T(8,128)(2,1)} %bitcast.10, bf16[192,256]{1,0:T(8,128)(2,1)} %bitcast.11, bf16[192,512]{1,0:T(8,128)(2,1)} %w_h.1, s32[2,128]{1,0:T(2,128)} %bitcast.12), custom_call_target="tpu_custom_call" | custom-call | tf_op jit(solution)/shard_map/pallas_call | solution.py:428
  75.1 0.6 copy.12
  75.8 0.6 copy.13
  76.4 0.7 copy.14

commit v6 on v5

--- a/solution.py
+++ b/solution.py
@@ -337,20 +337,20 @@
         me = home[1 - h]
         k2c += [send(k2s.at[h, turn[1 - h](d)], k2.at[h, me], first[h][d]) for d in NEAR]
         k2[h, me] = k2s[h, me]
-    tpt = 2 * oxlo + c
     for dr in range(2):
         zc[dr, 2].wait_recv()
     for n in range(2):
         for dr in range(2):
             zc[dr, 3, n].wait_recv()
-    q1, q2 = [], []
+    q1, q2, q3 = [], [], []
     for h in range(2):
         dq4[t, H[h], :] = (dqf[0, H[h], :] + add_all(
             [zr[dr, i, H[h], :].astype(F32) for dr in range(2) for i in (2, 3)])).astype(BF16)
         r = dq4.at[t, H[h]]
         q1.append(send(r, r, partner))
         q2.append(send(r, r, core_dev))
-    d1, d2 = [], []
+        q3.append(send(r, r, cross))
+    d1, d2, d3 = [], [], []
     for h in range(2):
         for cp in k2c[3 * h:3 * h + 3]:
             cp.wait_recv()
@@ -358,21 +358,12 @@
         r = dk4.at[t, H[h]]
         d1.append(send(r, r, partner))
         d2.append(send(r, r, core_dev))
-    q3 = []
-    for h in range(2):
-        q1[h].wait_recv()
-        r = dq4.at[tpt, H[h]]
-        q3.append(send(r, r, core_dev))
-    d3 = []
-    for h in range(2):
-        d1[h].wait_recv()
-        r = dk4.at[tpt, H[h]]
-        d3.append(send(r, r, core_dev))
-    for cp in q2 + q3:
+        d3.append(send(r, r, cross))
+    for cp in q1 + q2 + q3:
         cp.wait_recv()
     dq = dq4[...].reshape(ROWS, EMB)
     head = jnp.dot(xqt[...], dq, preferred_element_type=F32)
-    for cp in d2 + d3:
+    for cp in d1 + d2 + d3:
         cp.wait_recv()
     dkv = dk4[...].reshape(ROWS, EMB)
     head += jnp.dot(xkt[...], dkv, preferred_element_type=F32)

time: 79.1 us -> 78.5 us (level)
  no operation moved by 1% of the time
where the time goes in v6:
time: 78.5 us; the launch traced here: 78.4 us
  Pallas kernels  74.5 us (95%)
  local copies, waits for them, and re-layouts  2.03 us (3%)
  between operations  1.81 us (2%)
    pallas_call x1, Pallas kernels, body(): pl.pallas_call(kernel, out_shape=(jax.ShapeDtypeStruct((1, 128), F32), V(...  74.5 us
    unnamed x3, local copies, waits for them, and re-layouts  2.03 us

profile of v6, /device:TPU:2, one launch (start us, length us, event | category | flops | bytes accessed | tf_op | source)
XLA Modules:
  0.0 78.4 jit_solution(317751819370168588)
XLA Ops:
  0.6 74.5 %shard_map.75 = (f32[1,128]{1,0:T(1,128)S(1)}, bf16[192,256]{1,0:T(8,128)(2,1)S(1)}, bf16[192,256]{1,0:T(8,128)(2,1)S(1)}, f32[192,512]{1,0:T(8,128)S(1)}) custom-call(bf16[192,256]{1,0:T(8,128)(2,1)} %bitcast.10, bf16[192,256]{1,0:T(8,128)(2,1)} %bitcast.11, bf16[192,512]{1,0:T(8,128)(2,1)} %w_h.1, s32[2,128]{1,0:T(2,128)} %bitcast.12), custom_call_target="tpu_custom_call" | custom-call | tf_op jit(solution)/shard_map/pallas_call | solution.py:419
  75.2 0.6 copy.12
  75.8 0.6 copy.13
  76.4 0.7 copy.14
